TPU v7x, 512 devices: a whole 4x4x16 slice. The times are simulated.
512 devices in a mesh: dp: 32 (over z, core), dap: 16 (over x, y).
Axes of the slice: x: 4, y: 4, z: 16, core: 2. Of those that a mesh axis runs over, the one named last changes fastest.
Arguments:
- pair: bfloat16 [32, 192, 192, 128], P('dp', 'dap'), may hold values from -60 to 60
- pair_cot: bfloat16 [32, 192, 192, 128], P('dp', 'dap'), may hold values from -6 to 6
- residue_mask: int32 [32, 192], P('dp'), may hold values from 0 to 1, as said below
- w_in: bfloat16 [2, 128, 640], replicated, may hold values from -0.5 to 0.5
- w_out: bfloat16 [2, 128, 128], replicated, may hold values from -0.5 to 0.5
Outputs:
- pair_grad: bfloat16 [32, 192, 192, 128], P('dp', 'dap')
- w_in_grad: float32 [2, 128, 640], replicated
- w_out_grad: float32 [2, 128, 128], replicated
Inputs may be any that keep to these rules, and one draw needn't show every extreme that they name: `residue_mask`: in each crop the real residues form a prefix of its 192 residues that holds at least half of them; the rest are 0.
All inputs are finite; a program needn't handle non-finite values.
Results may differ from a plain program's by a relative error of at most 0.019.
Values may be sent and summed in bfloat16 or wider, within the bound.
A program may use at most 192 MiB of HBM per device.

v0:
```python
import jax
import jax.numpy as jnp
from jax import lax
from jax.sharding import PartitionSpec as P

EPS = 1e-05


def normal_form(values):
    average = jnp.mean(values, -1, keepdims=True)
    centred = values - average
    inv_std = lax.rsqrt(jnp.mean(centred * centred, -1, keepdims=True) + EPS)
    return (centred * inv_std, inv_std)


def norm_back(grad, normed, inv_std):
    return inv_std * (
        grad
        - jnp.mean(grad, -1, keepdims=True)
        - normed * jnp.mean(grad * normed, -1, keepdims=True)
    )


def gated_pair(projected, pair_mask, hidden):
    left_value = projected[..., :hidden]
    left_gate = jax.nn.sigmoid(projected[..., hidden : 2 * hidden])
    right_value = projected[..., 2 * hidden : 3 * hidden]
    right_gate = jax.nn.sigmoid(projected[..., 3 * hidden : 4 * hidden])
    left = (left_gate * left_value * pair_mask).astype(jnp.bfloat16)
    right = (right_gate * right_value * pair_mask).astype(jnp.bfloat16)
    return (left, right, (left_value, left_gate, right_value, right_gate))


def half_back(grad, value, gate, pair_mask):
    return jnp.concatenate(
        [grad * gate * pair_mask, grad * value * pair_mask * gate * (1.0 - gate)], -1
    )


def product(first, second, form):
    return jnp.einsum(form, first, second, preferred_element_type=jnp.float32)


def local(pair, pair_cot, residue_mask, w_in, w_out):
    row_count = pair.shape[1]
    length = pair.shape[2]
    hidden = w_out.shape[1]
    split_at = 4 * hidden
    residues = residue_mask[0].astype(jnp.float32)
    own_valid = lax.dynamic_slice_in_dim(residues, lax.axis_index("dap") * row_count, row_count)
    pair_mask = (own_valid[:, None] * residues[None, :])[:, :, None]
    first_in = w_in[0]
    second_in = w_in[1]
    first_out = w_out[0]
    second_out = w_out[1]
    pair_one = pair[0]
    one_normed, one_inv = normal_form(pair_one.astype(jnp.float32))
    one_zed = one_normed.astype(jnp.bfloat16)
    one_proj = product(one_zed, first_in, "ijc,cd->ijd")
    left_one, right_one, stored_one = gated_pair(one_proj[..., :split_at], pair_mask, hidden)
    gate_one = jax.nn.sigmoid(one_proj[..., split_at:])
    right_one_all = lax.all_gather(right_one, "dap", axis=0, tiled=True)
    tri_one = product(left_one, right_one_all, "ikh,jkh->ijh")
    tri_one_normed, tri_one_inv = normal_form(tri_one)
    tri_one_zed = tri_one_normed.astype(jnp.bfloat16)
    result_one = product(tri_one_zed, first_out, "ijh,hc->ijc")
    pair_two = (pair_one.astype(jnp.float32) + gate_one * result_one).astype(jnp.bfloat16)
    column_two = jnp.transpose(
        lax.all_to_all(pair_two, "dap", split_axis=1, concat_axis=0, tiled=True), (1, 0, 2)
    )
    src_normed, src_inv = normal_form(column_two.astype(jnp.float32))
    src_zed = src_normed.astype(jnp.bfloat16)
    left_two, right_two, stored_two = gated_pair(
        product(src_zed, second_in[:, :split_at], "ijc,cd->ijd"), pair_mask, hidden
    )
    two_normed, two_inv = normal_form(pair_two.astype(jnp.float32))
    two_zed = two_normed.astype(jnp.bfloat16)
    gate_two = jax.nn.sigmoid(product(two_zed, second_in[:, split_at:], "ijc,cd->ijd"))
    right_two_all = lax.all_gather(right_two, "dap", axis=0, tiled=True)
    tri_two = product(left_two, right_two_all, "ikh,jkh->ijh")
    tri_two_normed, tri_two_inv = normal_form(tri_two)
    tri_two_zed = tri_two_normed.astype(jnp.bfloat16)
    result_two = product(tri_two_zed, second_out, "ijh,hc->ijc")
    upstream = pair_cot[0].astype(jnp.float32)
    grad_result_two = (upstream * gate_two).astype(jnp.bfloat16)
    grad_gate_two = (upstream * result_two * gate_two * (1.0 - gate_two)).astype(jnp.bfloat16)
    grad_tri_two = norm_back(
        product(grad_result_two, second_out, "ijc,hc->ijh"), tri_two_normed, tri_two_inv
    ).astype(jnp.bfloat16)
    out_grad_two = product(tri_two_zed, grad_result_two, "ijh,ijc->hc")
    grad_left_two = product(grad_tri_two, right_two_all, "ijh,jkh->ikh")
    tri_columns = lax.all_to_all(grad_tri_two, "dap", split_axis=1, concat_axis=0, tiled=True)
    section = tri_columns
    grad_right_two = product(
        section, lax.all_gather(left_two, "dap", axis=0, tiled=True), "ijh,ikh->jkh"
    )
    src_proj = jnp.concatenate(
        [
            half_back(grad_left_two, stored_two[0], stored_two[1], pair_mask),
            half_back(grad_right_two, stored_two[2], stored_two[3], pair_mask),
        ],
        -1,
    ).astype(jnp.bfloat16)
    src_weight = second_in[:, :split_at]
    own_weight = second_in[:, split_at:]
    src_grad = norm_back(product(src_proj, src_weight, "ijd,cd->ijc"), src_normed, src_inv)
    returned = lax.all_to_all(
        jnp.transpose(src_grad, (1, 0, 2)).astype(jnp.bfloat16),
        "dap",
        split_axis=0,
        concat_axis=1,
        tiled=True,
    ).astype(jnp.float32)
    own_grad = norm_back(product(grad_gate_two, own_weight, "ijd,cd->ijc"), two_normed, two_inv)
    in_grad_two = jnp.concatenate(
        [product(src_zed, src_proj, "ijc,ijd->cd"), product(two_zed, grad_gate_two, "ijc,ijd->cd")],
        1,
    )
    upstream_one = (upstream + own_grad + returned).astype(jnp.bfloat16).astype(jnp.float32)
    grad_result_one = (upstream_one * gate_one).astype(jnp.bfloat16)
    grad_gate_one = (upstream_one * result_one * gate_one * (1.0 - gate_one)).astype(jnp.bfloat16)
    grad_tri_one = norm_back(
        product(grad_result_one, first_out, "ijc,hc->ijh"), tri_one_normed, tri_one_inv
    ).astype(jnp.bfloat16)
    out_grad_one = product(tri_one_zed, grad_result_one, "ijh,ijc->hc")
    grad_left_one = product(grad_tri_one, right_one_all, "ijh,jkh->ikh")
    tri_one_columns = lax.all_to_all(grad_tri_one, "dap", split_axis=1, concat_axis=0, tiled=True)
    section = tri_one_columns
    grad_right_one = product(
        section, lax.all_gather(left_one, "dap", axis=0, tiled=True), "ijh,ikh->jkh"
    )
    factor_grads = jnp.concatenate(
        [
            half_back(grad_left_one, stored_one[0], stored_one[1], pair_mask),
            half_back(grad_right_one, stored_one[2], stored_one[3], pair_mask),
        ],
        -1,
    ).astype(jnp.bfloat16)
    grad_proj_one = jnp.concatenate([factor_grads, grad_gate_one], -1)
    one_grad = norm_back(product(grad_proj_one, first_in, "ijd,cd->ijc"), one_normed, one_inv)
    pair_grad = (upstream_one + one_grad).astype(jnp.bfloat16)[None]
    in_grad_one = product(one_zed, grad_proj_one, "ijc,ijd->cd")
    in_total, out_total = lax.psum(
        (jnp.stack([in_grad_one, in_grad_two]), jnp.stack([out_grad_one, out_grad_two])),
        ("dp", "dap"),
    )
    return (pair_grad, in_total / length, out_total / length)


def solution(mesh):
    return jax.shard_map(
        local,
        mesh=mesh,
        in_specs=(P("dp", "dap", None, None), P("dp", "dap", None, None), P("dp", None), P(), P()),
        out_specs=(P("dp", "dap", None, None), P(), P()),
        check_vma=False,
    )
```

profile of v0, /device:TPU:1, one launch (start us, length us, event | category | flops | bytes accessed | tf_op | source)
XLA Modules:
  0.0 1015.7 jit_solution(2720904409827335183)
XLA Ops:
  13.9 3.5 multiply_convert_fusion.4
  20.5 93.5 %all-gather.5.cloned.1.call-done = bf16[192,192,128]{2,1,0:T(8,128)(2,1)} async-done(((bf16[12,192,128]{2,1,0:T(8,128)(2,1)}), bf16[192,192,128]{2,1,0:T(8,128)(2,1)}) %all-gather.5.cloned.1.call-update) | async-done | bytes 9437200 | tf_op jit(solution)/shard_map/all_gather | solution.py:62
  114.0 17.4 %copy.97 = bf16[192,192,128]{1,0,2:T(8,128)(2,1)} copy(bf16[192,192,128]{2,1,0:T(8,128)(2,1)} %all-gather.5.cloned.1.call-done) | data formatting | bytes 18874368 | tf_op jit(solution)/shard_map/all_gather | solution.py:62
  131.4 8.6 bitcast_reduce_fusion.1
  143.9 3.6 convert_reduce_fusion.1
  149.7 4.6 all-to-all-start
  154.4 12.7 %all-to-all-done = bf16[12,192,128]{2,0,1:T(8,128)(2,1)} async-done(((bf16[12,192,128]{2,0,1:T(8,128)(2,1)}), bf16[12,192,128]{2,0,1:T(8,128)(2,1)}, u32[]{:S(2)}, u32[]{:S(2)}) %all-to-all-start) | async-done | bytes 589856 | tf_op jit(solution)/shard_map/all_to_all | solution.py:69
  169.9 3.3 copy.102
  191.2 17.3 %all-gather.11.cloned.1.call-done = bf16[192,192,128]{2,1,0:T(8,128)(2,1)} async-done(((bf16[12,192,128]{2,1,0:T(8,128)(2,1)}), bf16[192,192,128]{2,1,0:T(8,128)(2,1)}) %all-gather.11.cloned.1.call-update) | async-done | bytes 9437200 | tf_op jit(solution)/shard_map/all_gather | solution.py:130
  208.5 17.3 %copy.126 = bf16[192,192,128]{1,0,2:T(8,128)(2,1)} copy(bf16[192,192,128]{2,1,0:T(8,128)(2,1)} %all-gather.11.cloned.1.call-done) | data formatting | bytes 18874368 | tf_op jit(solution)/shard_map/all_gather | solution.py:130
  229.8 73.2 %all-gather.7.cloned.1.call-done = bf16[192,192,128]{2,1,0:T(8,128)(2,1)} async-done(((bf16[12,192,128]{2,1,0:T(8,128)(2,1)}), bf16[192,192,128]{2,1,0:T(8,128)(2,1)}) %all-gather.7.cloned.1.call-update) | async-done | bytes 9437200 | tf_op jit(solution)/shard_map/all_gather | solution.py:79
  302.9 17.4 %copy.103 = bf16[192,192,128]{1,0,2:T(8,128)(2,1)} copy(bf16[192,192,128]{2,1,0:T(8,128)(2,1)} %all-gather.7.cloned.1.call-done) | data formatting | bytes 18874368 | tf_op jit(solution)/shard_map/all_gather | solution.py:79
  320.3 10.7 %bitcast_reduce_fusion = (f32[12,192]{1,0:T(8,128)}, f32[128,192,12]{1,2,0:T(8,128)}) fusion(bf16[192,192,128]{1,0,2:T(8,128)(2,1)} %copy.103, bf16[12,192,128]{1,0,2:T(8,128)(2,1)} %copy.104), kind=kOutput, calls=%fused_computation.2 | convolution fusion | flops 113538816 | bytes 11215872 | tf_op jit(solution)/shard_map/ikh,jkh->ijh/dot_general | solution.py:41
  333.8 3.3 fusion.2
  341.7 4.8 all-to-all-start.1
  351.9 8.6 fusion.138
  360.5 3.5 fusion.133
  366.8 32.0 %all-gather.9.cloned.1.call-done = bf16[192,192,128]{2,1,0:T(8,128)(2,1)} async-done(((bf16[12,192,128]{2,1,0:T(8,128)(2,1)}), bf16[192,192,128]{2,1,0:T(8,128)(2,1)}) %all-gather.9.cloned.1.call-update) | async-done | bytes 9437200 | tf_op jit(solution)/shard_map/all_gather | solution.py:95
  398.8 17.4 %copy.113 = bf16[192,192,128]{1,0,2:T(8,128)(2,1)} copy(bf16[192,192,128]{2,1,0:T(8,128)(2,1)} %all-gather.9.cloned.1.call-done) | data formatting | bytes 18874368 | tf_op jit(solution)/shard_map/all_gather | solution.py:95
  427.0 7.9 fusion.139
  437.6 3.8 fusion.78
  446.0 4.5 all-to-all-start.2
  456.1 7.2 all-to-all-done.2
  465.7 3.3 copy.118
  471.6 3.3 fusion.39
  482.0 7.7 fusion.140
  496.3 4.6 all-to-all-start.3
  506.8 6.6 all-to-all-done.3
  514.8 6.3 fusion.141
  530.6 3.2 fusion.132
  533.9 3.3 convolution_bitcast_fusion
  540.5 465.5 %all-reduce.3.cloned.1.call-done = (f32[2,128,640]{2,1,0:T(8,128)}, f32[2,128,128]{2,1,0:T(8,128)}) async-done(((f32[2,128,640]{2,1,0:T(8,128)}, f32[2,128,128]{2,1,0:T(8,128)}), (f32[2,128,640]{2,1,0:T(8,128)}, f32[2,128,128]{2,1,0:T(8,128)})) %all-reduce.3.cloned.1.call-update) | async-done | bytes 786448 | tf_op jit(solution)/shard_map/psum | solution.py:143
  (182 shorter events, 120.7 us)
Async XLA Ops:
  7.2 3.5 copy-start.4
  7.2 3.4 copy-start.43
  7.2 3.4 copy-start.25
  7.2 106.8 %all-gather.5.cloned.1.call-start = ((), (), s32[]{:S(2)}) async-start(), calls=%async_computation.4 | async-start | bytes 10027008 | tf_op jit(solution)/shard_map/all_gather | solution.py:62
  17.5 191.0 %all-gather.11.cloned.1.call-start = ((), (), s32[]{:S(2)}) async-start(), calls=%async_computation.7 | async-start | bytes 10027008 | tf_op jit(solution)/shard_map/all_gather | solution.py:130
  143.9 3.6 copy-start.23
  148.4 6.0 copy-start.26
  149.7 17.4 %all-to-all-start = ((bf16[12,192,128]{2,0,1:T(8,128)(2,1)}), bf16[12,192,128]{2,0,1:T(8,128)(2,1)}, u32[]{:S(2)}, u32[]{:S(2)}) async-start(bf16[12,192,128]{2,0,1:T(8,128)(2,1)} %copy.100), calls=%async_computation | async-start | bytes 1572864 | tf_op jit(solution)/shard_map/all_to_all | solution.py:69
  154.3 148.7 %all-gather.7.cloned.1.call-start = ((), (), s32[]{:S(2)}) async-start(), calls=%async_computation.5 | async-start | bytes 10027008 | tf_op jit(solution)/shard_map/all_gather | solution.py:79
  178.0 2.6 copy-start
  180.6 218.3 %all-gather.9.cloned.1.call-start = ((), (), s32[]{:S(2)}) async-start(), calls=%async_computation.6 | async-start | bytes 10027008 | tf_op jit(solution)/shard_map/all_gather | solution.py:95
  331.0 2.8 copy-start.1
  333.8 3.3 copy-start.2
  333.8 3.3 copy-start.42
  341.7 78.5 %all-to-all-start.1 = ((bf16[12,192,128]{2,0,1:T(8,128)(2,1)}), bf16[12,192,128]{2,0,1:T(8,128)(2,1)}, u32[]{:S(2)}, u32[]{:S(2)}) async-start(bf16[12,192,128]{2,0,1:T(8,128)(2,1)} %copy.110), calls=%async_computation.1 | async-start | bytes 1572864 | tf_op jit(solution)/shard_map/all_to_all | solution.py:92
  437.6 3.8 copy-start.36
  444.6 5.8 copy-start.30
  446.0 17.3 %all-to-all-start.2 = ((bf16[192,12,128]{2,1,0:T(8,128)(2,1)}), bf16[192,12,128]{2,1,0:T(8,128)(2,1)}, u32[]{:S(2)}, u32[]{:S(2)}) async-start(bf16[192,12,128]{2,1,0:T(8,128)(2,1)} %copy.116), calls=%async_computation.2 | async-start | bytes 1572864 | tf_op jit(solution)/shard_map/all_to_all | solution.py:107
  469.1 2.5 copy-start.8
  469.1 2.5 copy-start.10
  469.1 2.5 copy-start.40
  469.1 2.5 copy-start.41
  471.6 3.3 copy-start.34
  496.3 5.0 copy-start.13
  496.3 5.0 copy-start.24
  496.3 17.0 %all-to-all-start.3 = ((bf16[12,192,128]{2,0,1:T(8,128)(2,1)}), bf16[12,192,128]{2,0,1:T(8,128)(2,1)S(1)}, u32[]{:S(2)}, u32[]{:S(2)}) async-start(bf16[12,192,128]{2,0,1:T(8,128)(2,1)} %copy.123), calls=%async_computation.3 | async-start | bytes 1572864 | tf_op jit(solution)/shard_map/all_to_all | solution.py:127
  501.0 505.0 %all-reduce.3.cloned.1.call-start = ((), (), s32[]{:S(2)}) async-start(), calls=%async_computation.8 | async-start | bytes 1572864 | tf_op jit(solution)/shard_map/psum | solution.py:143
  524.8 3.2 copy-start.14
  524.8 3.2 copy-start.16
  528.0 2.6 copy-start.5
  528.0 2.6 copy-start.27
  533.9 3.4 copy-start.15
  (21 other events, 39.4 us)
Sparse Core Ops, SparseCore 0:
  17.6 96.3 all-gather.4
  117.6 90.7 all-gather.10
  212.1 90.7 all-gather.6
  305.9 92.9 all-gather.8
  538.3 467.6 all-reduce.2
where the time goes:
time: 1030 us; the launch traced here: 1020 us
  waiting for transfers between devices  709 us (69%)
  local copies, waits for them, and re-layouts  124 us (12%)
  matrix products  87.5 us (8%)
  other arithmetic  61.3 us (6%)
  starting transfers between devices  19.6 us (2%)
  between operations  15 us (1%)
    psum x1, waiting for transfers between devices, local(): lax.psum((jnp.stack([in_grad_one, in_grad_two]), jnp.stack([out_grad_one,...  465 us
    all_gather x1, waiting for transfers between devices, local(): right_one_all = lax.all_gather(right_one, 'dap', axis=0, tiled=True)  93.5 us
    dot_general x21, matrix products, product(): return jnp.einsum(form, first, second, preferred_element_type=jnp.float32)  87.5 us
    all_gather x1, waiting for transfers between devices, local(): right_two_all = lax.all_gather(right_two, 'dap', axis=0, tiled=True)  73.2 us
    all_gather x1, waiting for transfers between devices, local(): lax.all_gather(left_two, 'dap', axis=0, tiled=True)  32 us
  transfers between devices with their start and end apart: 9, of which 8 were waited for; matrix products, arithmetic and copies ran while one was open for 17% of the time, Pallas kernels for 0%

commit v1 on v0

v1 whole, which is shorter than its diff:
```python
import functools

import jax
import jax.numpy as jnp
from jax import lax
from jax.experimental import pallas as pl
from jax.experimental.pallas import tpu as pltpu
from jax.sharding import PartitionSpec as P

EPS = 1e-05
D = 16
R = 12
N = 192
C = 128
CH = 6
W = 2 * N
ROWS = 5 * C + C
PART = ROWS // D
f32 = jnp.float32
bf16 = jnp.bfloat16
MESH = pl.DeviceIdType.MESH


def dot(a, b, ca, cb):
    return lax.dot_general(a, b, (((ca,), (cb,)), ((), ())), preferred_element_type=f32)


def normal_form(x):
    centred = x - jnp.mean(x, 0, keepdims=True)
    inv = lax.rsqrt(jnp.mean(centred * centred, 0, keepdims=True) + EPS)
    return centred * inv, inv


def norm_back(d, n, inv):
    return inv * (d - jnp.mean(d, 0, keepdims=True) - n * jnp.mean(d * n, 0, keepdims=True))


def kernel(
    ndp,
    pair_ref, cot_ref, mask_ref, wt_ref, wp_ref, wo_ref, wot_ref,
    out_ref, gin_ref, gout_ref,
    n_ref, inv_ref, z_ref, v_ref, sg_ref, gate_ref, res_ref, ntri_ref, itri_ref, xz_ref,
    p_ref, up_ref, dres_ref, dq_ref, lm_ref, tm_ref, a_ref, b_ref,
    big_send, small_send, big_recv, small_recv,
    grads, rs_recv, dp_send, dp_recv, dp_all, fin_all,
    ssem, rsem, lsem, dps, dpr,
):
    me = lax.axis_index("dap")
    my = lax.axis_index("dp")

    barrier = pltpu.get_barrier_semaphore()

    @pl.loop(1, D)
    def _(k):
        pl.semaphore_signal(barrier, inc=1, device_id={"dap": lax.rem(me + k, D)}, device_id_type=MESH)

    @pl.loop(1, ndp)
    def _(k):
        pl.semaphore_signal(barrier, inc=1, device_id={"dp": lax.rem(my + k, ndp)}, device_id_type=MESH)

    count = jnp.sum(mask_ref[...].astype(f32), 1, keepdims=True)

    def cell_mask(c):
        lane = lax.broadcasted_iota(jnp.int32, (1, W), 1)
        second = ((lane >= C) & (lane < 2 * C)) | (lane >= 2 * C + 64)
        k = jnp.where(lane < C, lane, jnp.where(lane < 2 * C + 64, lane - C, lane - N))
        k = jnp.where((lane >= C) & (lane < 2 * C), lane - C, k)
        row = me * R + 2 * c + second.astype(jnp.int32)
        return jnp.where((jnp.maximum(k, row).astype(f32) < count), 1.0, 0.0).astype(f32)

    def load_cells(ref, c):
        i = 2 * c
        x = jnp.concatenate(
            [ref[i, 0:C], ref[i + 1, 0:C], ref[i, C:N], ref[i + 1, C:N]], 0
        )
        return jnp.transpose(x.astype(f32))

    def copy_of(send, recv, phase, peer, slot, src):
        return pltpu.make_async_remote_copy(
            src_ref=send.at[peer],
            dst_ref=recv.at[slot],
            send_sem=ssem.at[phase, peer],
            recv_sem=rsem.at[phase, src],
            device_id={"dap": peer},
            device_id_type=MESH,
        )

    def send_to(send, recv, phase, peer):
        copy_of(send, recv, phase, peer, me, me).start()

    def own_copy(send, recv):
        return pltpu.make_async_copy(send.at[me], recv.at[me], lsem)

    def wait_from(send, recv, phase, src):
        copy_of(send, recv, phase, src, src, src).wait_recv()

    def send_all(send, recv, phase):
        own_copy(send, recv).start()

        @pl.loop(1, D)
        def _(k):
            send_to(send, recv, phase, lax.rem(me + k, D))

    def wait_sends(send, recv, phase):
        @pl.loop(1, D)
        def _(k):
            copy_of(send, recv, phase, lax.rem(me + k, D), me, me).wait_send()

    def wait_all(send, recv, phase):
        own_copy(send, recv).wait()

        @pl.loop(1, D)
        def _(k):
            wait_from(send, recv, phase, lax.rem(me + D - k, D))

    def project(u, c, x):
        n, inv = normal_form(x)
        n_ref[u, c] = n
        inv_ref[u, c] = inv
        z = n.astype(bf16)
        z_ref[u, c] = z
        mask = cell_mask(c)
        for g in range(2):
            v = dot(wt_ref[u, g * C : (g + 1) * C], z, 1, 0)
            sg = jax.nn.sigmoid(dot(wt_ref[u, (2 + g) * C : (3 + g) * C], z, 1, 0))
            v_ref[u, c, g * C : (g + 1) * C] = v
            sg_ref[u, c, g * C : (g + 1) * C] = sg
            lr = (sg * v * mask).astype(bf16)
            big_send[g * 8 : (g + 1) * 8, c] = lr.reshape(8, 16, W)
        gate_ref[u, c] = jax.nn.sigmoid(dot(wt_ref[u, 4 * C : 5 * C], z, 1, 0))

    def finish_product(u, c, t):
        n, inv = normal_form(t)
        ntri_ref[u, c] = n
        itri_ref[u, c] = inv
        xz = n.astype(bf16)
        xz_ref[u, c] = xz
        res = dot(wot_ref[u], xz, 1, 0)
        res_ref[u, c] = res
        return res

    def back_to_product(u, c, up):
        gate = gate_ref[u, c]
        dres = (up * gate).astype(bf16)
        dres_ref[u, c] = dres
        dq_ref[u, c, 4 * C : 5 * C] = (up * res_ref[u, c] * gate * (1.0 - gate)).astype(bf16)
        return norm_back(dot(wo_ref[u], dres, 1, 0), ntri_ref[u, c], itri_ref[u, c])

    def back_to_pair(u, c, slot):
        mask = cell_mask(c)
        for g in range(2):
            d = big_recv[slot, g * 8 : (g + 1) * 8, c].reshape(C, W).astype(f32)
            sg = sg_ref[u, c, g * C : (g + 1) * C]
            dv = d * sg * mask
            dq_ref[u, c, g * C : (g + 1) * C] = dv.astype(bf16)
            dg = dv * v_ref[u, c, g * C : (g + 1) * C] * (1.0 - sg)
            dq_ref[u, c, (2 + g) * C : (3 + g) * C] = dg.astype(bf16)
        d = dot(wp_ref[u], dq_ref[u, c], 1, 0)
        return norm_back(d, n_ref[u, c], inv_ref[u, c])

    def halves(slot, p):
        x = small_recv[slot, :, p].astype(f32).reshape(D, 2, 8, W)
        return x[:, 0].reshape(C, W), x[:, 1].reshape(C, W)

    def put_halves(p, pieces):
        both = [y.reshape(D, 1, 8, W) for y in pieces]
        small_send[:, p] = jnp.concatenate(both, 1).reshape(D, 16, W).astype(bf16)

    def in_grad(u):
        def step(c, acc):
            return acc + dot(dq_ref[u, c], z_ref[u, c], 1, 1)

        acc = lax.fori_loop(0, CH, step, jnp.zeros((5 * C, C), f32))
        for k in range(5 * C // 16):
            r = k * 16
            grads[r // PART, u, r % PART : r % PART + 16] = acc[r : r + 16]

    def out_grad(u):
        def step(c, acc):
            return acc + dot(xz_ref[u, c], dres_ref[u, c], 1, 1)

        acc = lax.fori_loop(0, CH, step, jnp.zeros((C, C), f32))
        for k in range(C // 16):
            r = 5 * C + k * 16
            grads[r // PART, u, r % PART : r % PART + 16] = acc[k * 16 : k * 16 + 16]

    def spread(x, row, step):
        a_ref[pl.ds(row, step)] = x[:, 0:C]
        a_ref[pl.ds(row + step, step)] = x[:, C : 2 * C]
        tail = x[:, 2 * C : W]
        b_ref[pl.ds(row, step)] = tail
        b_ref[pl.ds(row + step, step)] = pltpu.roll(tail, 64, 1)

    def collect(row, step):
        lane = lax.broadcasted_iota(jnp.int32, (step, C), 1)
        tail = jnp.where(lane < 64, b_ref[pl.ds(row, step)], b_ref[pl.ds(row + step, step)])
        return jnp.concatenate([a_ref[pl.ds(row, step)], a_ref[pl.ds(row + step, step)], tail], 1)

    def get_channel(ch, step):
        a = a_ref[pl.ds(ch, N, stride=step), :]
        b = b_ref[pl.ds(ch, N, stride=step), :]
        return a.astype(bf16), b[:, :64].astype(bf16)

    def put_channel(ch, step, x):
        a_ref[pl.ds(ch, N, stride=step), :] = x[:, 0:C]
        b_ref[pl.ds(ch, N, stride=step), :] = jnp.concatenate([x[:, C:N], x[:, C:N]], 1)

    def arrive(send, recv, phase, k):
        src = lax.rem(me + D - k, D)

        @pl.when(k == 0)
        def _():
            own_copy(send, recv).wait()

        @pl.when(k > 0)
        def _():
            wait_from(send, recv, phase, src)

        return src

    def depart(send, recv, phase, k):
        peer = lax.rem(me + k, D)

        @pl.when(k == 0)
        def _():
            own_copy(send, recv).start()

        @pl.when(k > 0)
        def _():
            send_to(send, recv, phase, peer)

    def products(u, phase, slot):
        recv = big_recv.at[slot]

        @pl.loop(0, D)
        def _(k):
            src = arrive(big_send, recv, phase, k)
            for c in range(CH):
                spread(big_recv[slot, src, c].astype(f32), (src * R + 2 * c) * 16, 16)

        for ch in range(16):
            a, b = get_channel(ch, 16)
            lm_ref[u, ch, :, 0:C] = a
            lm_ref[u, ch, :, C:N] = b
        for ch in range(8):
            left, right = lm_ref[u, ch], lm_ref[u, 8 + ch]
            axis = 1 - u
            put_channel(ch, 8, dot(left, right, axis, axis))

        @pl.loop(0, D)
        def _(k):
            peer = lax.rem(me + k, D)
            for p in range(CH // 2):
                row = (peer * R + 4 * p) * 8
                both = jnp.concatenate([collect(row, 8), collect(row + 16, 8)], 0)
                small_send[peer, p] = both.astype(bf16)
            depart(small_send, small_recv.at[slot], phase + 1, k)

    def product_grads(u, phase, slot):
        recv = small_recv.at[slot]

        @pl.loop(0, D)
        def _(k):
            src = arrive(small_send, recv, phase, k)
            for p in range(CH // 2):
                x = small_recv[slot, src, p].astype(f32)
                row = (src * R + 4 * p) * 8
                spread(x[0:8], row, 8)
                spread(x[8:16], row + 16, 8)

        for ch in range(8):
            a, b = get_channel(ch, 8)
            tm_ref[ch, :, 0:C] = a
            tm_ref[ch, :, C:N] = b
        for ch in range(8):
            left, right, grad = lm_ref[u, ch], lm_ref[u, 8 + ch], tm_ref[ch]
            if u == 0:
                dleft, dright = dot(grad, right, 1, 0), dot(grad, left, 0, 0)
            else:
                dleft, dright = dot(right, grad, 1, 1), dot(left, grad, 1, 0)
            put_channel(ch, 16, dleft)
            put_channel(8 + ch, 16, dright)

        @pl.loop(0, D)
        def _(k):
            peer = lax.rem(me + k, D)
            for c in range(CH):
                big_send[peer, c] = collect((peer * R + 2 * c) * 16, 16).astype(bf16)
            depart(big_send, big_recv.at[slot], phase + 1, k)

    @pl.loop(0, CH)
    def _(c):
        project(0, c, load_cells(pair_ref, c))

    pl.semaphore_wait(barrier, D - 1 + ndp - 1)
    send_all(big_send, big_recv.at[0], 0)
    products(0, 0, 0)
    wait_sends(big_send, big_recv.at[0], 0)
    wait_all(small_send, small_recv.at[0], 1)

    @pl.loop(0, CH // 2)
    def _(p):
        for a, t in enumerate(halves(0, p)):
            c = 2 * p + a
            res = finish_product(0, c, t)
            one = (load_cells(pair_ref, c) + gate_ref[0, c] * res).astype(bf16)
            project(1, c, one.astype(f32))

    send_all(big_send, big_recv.at[1], 2)
    wait_sends(small_send, small_recv.at[0], 1)
    products(1, 2, 1)
    wait_sends(big_send, big_recv.at[1], 2)
    wait_all(small_send, small_recv.at[1], 3)
    wait_sends(small_send, small_recv.at[1], 3)

    @pl.loop(0, CH // 2)
    def _(p):
        pieces = []
        for a, t in enumerate(halves(1, p)):
            c = 2 * p + a
            finish_product(1, c, t)
            pieces.append(back_to_product(1, c, load_cells(cot_ref, c)))
        put_halves(p, pieces)

    send_all(small_send, small_recv.at[2], 4)
    out_grad(1)
    product_grads(1, 4, 2)
    wait_sends(small_send, small_recv.at[2], 4)
    wait_all(big_send, big_recv.at[2], 5)

    @pl.loop(0, CH // 2)
    def _(p):
        pieces = []
        for a in range(2):
            c = 2 * p + a
            up = load_cells(cot_ref, c) + back_to_pair(1, c, 2)
            up = up.astype(bf16)
            up_ref[c] = up
            pieces.append(back_to_product(0, c, up.astype(f32)))
        put_halves(p, pieces)

    send_all(small_send, small_recv.at[3], 6)
    wait_sends(big_send, big_recv.at[2], 5)
    in_grad(1)
    out_grad(0)
    product_grads(0, 6, 3)
    wait_sends(small_send, small_recv.at[3], 6)
    wait_all(big_send, big_recv.at[3], 7)

    @pl.loop(0, CH)
    def _(c):
        total = up_ref[c].astype(f32) + back_to_pair(0, c, 3)
        y = jnp.transpose(total).astype(bf16)
        i = 2 * c
        out_ref[i, 0:C] = y[0:C]
        out_ref[i + 1, 0:C] = y[C : 2 * C]
        out_ref[i, C:N] = y[2 * C : 2 * C + 64]
        out_ref[i + 1, C:N] = y[2 * C + 64 : W]

    in_grad(0)
    wait_sends(big_send, big_recv.at[3], 7)

    send_all(grads, rs_recv, 8)
    wait_all(grads, rs_recv, 8)

    def add(k, acc):
        return acc + rs_recv[k].reshape(2 * PART, C)

    total = lax.fori_loop(1, D, add, rs_recv[0].reshape(2 * PART, C))
    piece = 2 * PART // ndp
    for k in range(ndp):
        dp_send[k] = total[k * piece : (k + 1) * piece]

    def dp_copy(src, dst, stage, peer, slot, origin):
        return pltpu.make_async_remote_copy(
            src_ref=src,
            dst_ref=dst.at[slot],
            send_sem=dps.at[stage, peer],
            recv_sem=dpr.at[stage, origin],
            device_id={"dp": peer},
            device_id_type=MESH,
        )

    @pl.loop(1, ndp)
    def _(k):
        peer = lax.rem(my + k, ndp)
        dp_copy(dp_send.at[peer], dp_recv, 0, peer, my, my).start()

    dp_recv[my] = dp_send[my]

    @pl.loop(1, ndp)
    def _(k):
        peer = lax.rem(my + ndp - k, ndp)
        dp_copy(dp_send.at[peer], dp_recv, 0, peer, peer, peer).wait_recv()

    acc = dp_recv[0]
    for k in range(1, ndp):
        acc = acc + dp_recv[k]
    dp_all[my] = acc

    @pl.loop(1, ndp)
    def _(k):
        peer = lax.rem(my + k, ndp)
        dp_copy(dp_all.at[my], dp_all, 1, peer, my, my).start()

    @pl.loop(1, ndp)
    def _(k):
        peer = lax.rem(my + ndp - k, ndp)
        dp_copy(dp_all.at[peer], dp_all, 1, peer, peer, peer).wait_recv()

    whole = jnp.concatenate([dp_all[k] for k in range(ndp)], 0)
    fin_all[me] = (whole * (1.0 / N)).reshape(2, PART, C)

    def fin_copy(peer, slot):
        return pltpu.make_async_remote_copy(
            src_ref=fin_all.at[slot],
            dst_ref=fin_all.at[slot],
            send_sem=ssem.at[9, peer],
            recv_sem=rsem.at[9, slot],
            device_id={"dap": peer},
            device_id_type=MESH,
        )

    @pl.loop(1, D)
    def _(k):
        fin_copy(lax.rem(me + k, D), me).start()

    @pl.loop(1, D)
    def _(k):
        peer = lax.rem(me + D - k, D)
        fin_copy(peer, peer).wait_recv()

    for u in range(2):
        full = fin_all[:, u].reshape(ROWS, C)
        for t in range(2):
            part = full[t * 2 * C : (t + 1) * 2 * C].reshape(D, 2, 8, C)
            for s in range(2):
                at = (2 * s + t) * C
                gin_ref[u, :, at : at + C] = jnp.transpose(part[:, s].reshape(C, C))
        gin_ref[u, :, 4 * C : 5 * C] = jnp.transpose(full[4 * C : 5 * C])
        gout_ref[u] = full[5 * C : ROWS]

    wait_sends(grads, rs_recv, 8)

    @pl.loop(1, ndp)
    def _(k):
        peer = lax.rem(my + k, ndp)
        dp_copy(dp_send.at[peer], dp_recv, 0, peer, my, my).wait_send()
        dp_copy(dp_all.at[my], dp_all, 1, peer, my, my).wait_send()

    @pl.loop(1, D)
    def _(k):
        fin_copy(lax.rem(me + k, D), me).wait_send()


def local(ndp, pair, pair_cot, residue_mask, w_in, w_out):
    cols = w_in[..., : 4 * C].reshape(2, C, 2, 2, D, 8).transpose(0, 1, 3, 4, 2, 5).reshape(2, C, 4 * C)
    wp = jnp.concatenate([cols, w_in[..., 4 * C :]], -1)
    wt = jnp.swapaxes(wp, 1, 2)
    wot = jnp.swapaxes(w_out, 1, 2)
    vmem = pl.BlockSpec(memory_space=pltpu.VMEM)
    piece = 2 * PART // ndp
    scratch = [
        pltpu.VMEM((2, CH, C, W), f32),
        pltpu.VMEM((2, CH, 1, W), f32),
        pltpu.VMEM((2, CH, C, W), bf16),
        pltpu.VMEM((2, CH, 2 * C, W), f32),
        pltpu.VMEM((2, CH, 2 * C, W), f32),
        pltpu.VMEM((2, CH, C, W), f32),
        pltpu.VMEM((2, CH, C, W), f32),
        pltpu.VMEM((2, CH, C, W), f32),
        pltpu.VMEM((2, CH, 1, W), f32),
        pltpu.VMEM((2, CH, C, W), bf16),
        pltpu.VMEM((8, C), f32),
        pltpu.VMEM((CH, C, W), bf16),
        pltpu.VMEM((2, CH, C, W), bf16),
        pltpu.VMEM((2, CH, 5 * C, W), bf16),
        pltpu.VMEM((2, 16, N, N), bf16),
        pltpu.VMEM((8, N, N), bf16),
        pltpu.VMEM((N * 16, C), f32),
        pltpu.VMEM((N * 16, C), f32),
        pltpu.VMEM((D, CH, 16, W), bf16),
        pltpu.VMEM((D, CH // 2, 16, W), bf16),
        pltpu.VMEM((4, D, CH, 16, W), bf16),
        pltpu.VMEM((4, D, CH // 2, 16, W), bf16),
        pltpu.VMEM((D, 2, PART, C), f32),
        pltpu.VMEM((D, 2, PART, C), f32),
        pltpu.VMEM((ndp, piece, C), f32),
        pltpu.VMEM((ndp, piece, C), f32),
        pltpu.VMEM((ndp, piece, C), f32),
        pltpu.VMEM((D, 2, PART, C), f32),
        pltpu.SemaphoreType.DMA((10, D)),
        pltpu.SemaphoreType.DMA((10, D)),
        pltpu.SemaphoreType.DMA,
        pltpu.SemaphoreType.DMA((2, ndp)),
        pltpu.SemaphoreType.DMA((2, ndp)),
    ]
    grad, in_total, out_total = pl.pallas_call(
        functools.partial(kernel, ndp),
        out_shape=(
            jax.ShapeDtypeStruct((R, N, C), bf16),
            jax.ShapeDtypeStruct((2, C, 5 * C), f32),
            jax.ShapeDtypeStruct((2, C, C), f32),
        ),
        in_specs=[vmem] * 7,
        out_specs=(vmem, vmem, vmem),
        scratch_shapes=scratch,
        compiler_params=pltpu.CompilerParams(
            collective_id=0, has_side_effects=True, vmem_limit_bytes=60 * 1024 * 1024
        ),
    )(pair[0], pair_cot[0], residue_mask, wt, wp, w_out, wot)
    return grad[None], in_total, out_total


def solution(mesh):
    return jax.shard_map(
        functools.partial(local, mesh.shape["dp"]),
        mesh=mesh,
        in_specs=(P("dp", "dap", None, None), P("dp", "dap", None, None), P("dp", None), P(), P()),
        out_specs=(P("dp", "dap", None, None), P(), P()),
        check_vma=False,
    )
```

time: 1030 us -> 194 us (0.19); the launches traced: 1020 us -> 194 us
  waiting for transfers between devices: 709 us -> 0 us
  Pallas kernels: 0 us -> 184 us
  local copies, waits for them, and re-layouts: 124 us -> 8.13 us
  matrix products: 87.5 us -> 0 us
  other arithmetic: 61.3 us -> 0.78 us
  starting transfers between devices: 19.6 us -> 0 us
  between operations: 15 us -> 0.69 us
    psum x1 -> x0, waiting for transfers between devices: 465 us -> none  [local(): lax.psum((jnp.stack([in_grad_one, in_grad_two]), jnp.stack([out_grad_one,...]
    all_gather x4 -> x0, waiting for transfers between devices: 216 us -> none  [the longest x1 93.5 us: local(): right_one_all = lax.all_gather(right_one, 'dap', axis=0, tiled=True)]
    pallas_call x0 -> x1, Pallas kernels: none -> 184 us  [local(): pl.pallas_call(functools.partial(kernel, ndp), out_shape=(jax.ShapeDtypeS...]
    dot_general x21 -> x0, matrix products: 87.5 us -> none  [product(): return jnp.einsum(form, first, second, preferred_element_type=jnp.float32)]
    all_gather x4 -> x0, local copies, waits for them, and re-layouts: 69.5 us -> none  [the longest x1 17.4 us: local(): right_one_all = lax.all_gather(right_one, 'dap', axis=0, tiled=True)]
    convert_element_type x14 -> x0, local copies, waits for them, and re-layouts: 29.8 us -> none  [the longest x3 7.03 us: local(): returned = lax.all_to_all(jnp.transpose(src_grad, (1, 0, 2)).astype(jnp.b...]
    all_to_all x4 -> x0, waiting for transfers between devices: 26.5 us -> none  [the longest x1 12.7 us: local(): lax.all_to_all(pair_two, 'dap', split_axis=1, concat_axis=0, tiled=True)]
    convert_element_type x11 -> x0, other arithmetic: 19.9 us -> none  [the longest x1 3.55 us: gated_pair(): left = (left_gate * left_value * pair_mask).astype(jnp.bfloat16)]
  transfers between devices with their start and end apart: 9 -> 0, of which waited for: 8 -> 0; matrix products, arithmetic and copies ran while one was open for 17% -> 0% of each run, Pallas kernels for 0% -> 0%
where the time goes in v1:
time: 194 us
  Pallas kernels  184 us (95%)
  local copies, waits for them, and re-layouts  8.13 us (4%)
    pallas_call x1, Pallas kernels, local(): pl.pallas_call(functools.partial(kernel, ndp), out_shape=(jax.ShapeDtypeS...  184 us
    unnamed x11, local copies, waits for them, and re-layouts  5.41 us

profile of v1, /device:TPU:1, one launch (start us, length us, event | category | flops | bytes accessed | tf_op | source)
XLA Modules:
  0.0 193.9 jit_solution(6687717405797433799)
XLA Ops:
  0.6 0.0 copy-start.1
  0.6 0.8 copy-done.1
  1.5 0.7 copy.14
  2.2 0.0 slice-start.1
  2.2 0.9 slice-done.1
  3.2 0.2 copy.16
  3.4 0.0 slice-start
  3.4 0.1 copy.13
  3.6 0.7 slice-done
  4.2 0.8 pad_maximum_fusion
  5.0 0.9 copy.15.wt_ref
  5.9 184.3 %shard_map.76 = (bf16[12,192,128]{2,1,0:T(8,128)(2,1)}, f32[2,128,640]{2,1,0:T(8,128)}, f32[2,128,128]{2,1,0:T(8,128)}) custom-call(bf16[12,192,128]{2,1,0:T(8,128)(2,1)} %bitcast.12, bf16[12,192,128]{2,1,0:T(8,128)(2,1)} %bitcast.13, s32[1,192]{1,0:T(1,128)} %mask_ref.1, bf16[2,640,128]{2,1,0:T(8,128)(2,1)} %copy.15.wt_ref, ...), custom_call_target="tpu_custom_call" | custom-call | tf_op jit(solution)/shard_map/pallas_call | solution.py:498
  190.2 0.0 copy-start
  190.2 2.0 %copy.20 = bf16[1,12,192,128]{3,2,1,0:T(8,128)(2,1)} copy(bf16[1,12,192,128]{3,2,1,0:T(8,128)(2,1)} %bitcast.14) | data formatting | bytes 1179648
  192.2 0.0 copy-done
  192.2 0.0 copy-start.2
  192.2 0.8 copy.21
  193.0 0.2 copy-done.2
  193.2 0.7 copy.22
  (1 shorter events, 0.0 us)
Async XLA Ops:
  0.6 0.8 copy-start.1
  2.2 0.9 slice-start.1
  3.4 0.8 slice-start
  190.2 2.0 %copy-start = (f32[2,128,640]{2,1,0:T(8,128)S(1)}, f32[2,128,640]{2,1,0:T(8,128)}, u32[]{:S(2)}) copy-start(f32[2,128,640]{2,1,0:T(8,128)} %get-tuple-element.15) | copy-start | bytes 1966084
  192.2 1.0 copy-start.2

commit v2 on v1

v2 whole, which is shorter than its diff:
```python
import functools

import jax
import jax.numpy as jnp
from jax import lax
from jax.experimental import pallas as pl
from jax.experimental.pallas import tpu as pltpu
from jax.sharding import PartitionSpec as P

EPS = 1e-05
D = 16
R = 12
N = 192
C = 128
CH = 6
W = 2 * N
CELLS = R * N
EARLY = 8 * C
LATE = 4 * C
f32 = jnp.float32
bf16 = jnp.bfloat16
MESH = pl.DeviceIdType.MESH


def dot(a, b, ca, cb):
    return lax.dot_general(a, b, (((ca,), (cb,)), ((), ())), preferred_element_type=f32)


def normal_form(x):
    centred = x - jnp.mean(x, 0, keepdims=True)
    inv = lax.rsqrt(jnp.mean(centred * centred, 0, keepdims=True) + EPS)
    return centred * inv, inv


def norm_back(d, n, inv):
    return inv * (d - jnp.mean(d, 0, keepdims=True) - n * jnp.mean(d * n, 0, keepdims=True))


def kernel(
    ndp,
    pair_ref, cot_ref, mask_ref, win_ref, wo_ref,
    out_ref, gin_ref, gout_ref,
    wt_ref, wp_ref, wot_ref,
    n_ref, inv_ref, z_ref, v_ref, sg_ref, gate_ref, res_ref, ntri_ref, itri_ref, xz_ref,
    up_ref, dres_ref, dq_ref, lm_ref, tm_ref, a_ref, b_ref,
    big_send, small_send, big_recv, small_recv,
    early, late, early_in, late_in, half_out, half_in, z_early, z_late, early_all, late_all,
    ssem, rsem, lsem, core_s, core_r, zs, zr,
):
    me = lax.axis_index("dap")
    my = lax.axis_index("dp")
    core, zed, nz = lax.rem(my, 2), my // 2, ndp // 2
    mate = my + 1 - 2 * core

    def offset(k, sign):
        j = lax.rem(7 * k, D)
        a, b = j // 4, lax.rem(j, 4)
        dx, dy = a + core * (b - a), b + core * (a - b)
        return lax.rem(me // 4 + 4 + sign * dx, 4) * 4 + lax.rem(lax.rem(me, 4) + 4 + sign * dy, 4)

    def peer_of(k):
        return offset(k, 1)

    def src_of(k):
        return offset(k, -1)

    def z_peer(k):
        return 2 * lax.rem(zed + k, nz) + core

    barrier = pltpu.get_barrier_semaphore()

    @pl.loop(1, D)
    def _(k):
        pl.semaphore_signal(barrier, inc=1, device_id={"dap": peer_of(k)}, device_id_type=MESH)

    pl.semaphore_signal(barrier, inc=1, device_id={"dp": mate}, device_id_type=MESH)

    @pl.loop(1, nz)
    def _(k):
        pl.semaphore_signal(barrier, inc=1, device_id={"dp": z_peer(k)}, device_id_type=MESH)

    for u in range(2):
        wt = jnp.transpose(win_ref[u].astype(f32))
        pieces = []
        for t in range(2):
            both = [wt[(2 * e + t) * C : (2 * e + t + 1) * C].reshape(D, 1, 8, C) for e in range(2)]
            pieces.append(jnp.concatenate(both, 1).reshape(2 * C, C))
        wt = jnp.concatenate(pieces + [wt[4 * C : 5 * C]], 0)
        wt_ref[u] = wt.astype(bf16)
        wp_ref[u] = jnp.transpose(wt).astype(bf16)
        wot_ref[u] = jnp.transpose(wo_ref[u].astype(f32)).astype(bf16)

    count = jnp.sum(mask_ref[...].astype(f32), 1, keepdims=True)

    def cell_mask(c):
        lane = lax.broadcasted_iota(jnp.int32, (1, W), 1)
        second = ((lane >= C) & (lane < 2 * C)) | (lane >= 2 * C + 64)
        k = jnp.where(lane < C, lane, jnp.where(lane < 2 * C + 64, lane - C, lane - N))
        k = jnp.where((lane >= C) & (lane < 2 * C), lane - C, k)
        row = me * R + 2 * c + second.astype(jnp.int32)
        return jnp.where((jnp.maximum(k, row).astype(f32) < count), 1.0, 0.0).astype(f32)

    def cells(c):
        return pl.ds(pl.multiple_of(c * W, C), W)

    def load_cells(ref, c):
        i = 2 * c
        x = jnp.concatenate(
            [ref[i, 0:C], ref[i + 1, 0:C], ref[i, C:N], ref[i + 1, C:N]], 0
        )
        return jnp.transpose(x.astype(f32))

    def copy_of(send, recv, phase, peer, slot, src):
        return pltpu.make_async_remote_copy(
            src_ref=send.at[peer],
            dst_ref=recv.at[slot],
            send_sem=ssem.at[phase, peer],
            recv_sem=rsem.at[phase, src],
            device_id={"dap": peer},
            device_id_type=MESH,
        )

    def send_to(send, recv, phase, peer):
        copy_of(send, recv, phase, peer, me, me).start()

    def own_copy(send, recv, phase):
        return pltpu.make_async_copy(send.at[me], recv.at[me], lsem.at[phase])

    def wait_from(send, recv, phase, src):
        copy_of(send, recv, phase, src, src, src).wait_recv()

    def send_all(send, recv, phase):
        own_copy(send, recv, phase).start()

        @pl.loop(1, D)
        def _(k):
            send_to(send, recv, phase, peer_of(k))

    def wait_sends(send, recv, phase):
        @pl.loop(1, D)
        def _(k):
            copy_of(send, recv, phase, peer_of(k), me, me).wait_send()

    def wait_all(send, recv, phase):
        own_copy(send, recv, phase).wait()

        @pl.loop(1, D)
        def _(k):
            wait_from(send, recv, phase, src_of(k))

    def project(u, c, x):
        n, inv = normal_form(x)
        n_ref[u, c] = n
        inv_ref[u, c] = inv
        z = n.astype(bf16)
        z_ref[u, :, cells(c)] = z
        mask = cell_mask(c)
        for g in range(2):
            v = dot(wt_ref[u, g * C : (g + 1) * C], z, 1, 0)
            sg = jax.nn.sigmoid(dot(wt_ref[u, (2 + g) * C : (3 + g) * C], z, 1, 0))
            v_ref[u, c, g * C : (g + 1) * C] = v
            sg_ref[u, c, g * C : (g + 1) * C] = sg
            lr = (sg * v * mask).astype(bf16)
            big_send[g * 8 : (g + 1) * 8, c] = lr.reshape(8, 16, W)
        gate_ref[u, c] = jax.nn.sigmoid(dot(wt_ref[u, 4 * C : 5 * C], z, 1, 0))

    def finish_product(u, c, t):
        n, inv = normal_form(t)
        ntri_ref[u, c] = n
        itri_ref[u, c] = inv
        xz = n.astype(bf16)
        xz_ref[u, :, cells(c)] = xz
        res = dot(wot_ref[u], xz, 1, 0)
        res_ref[u, c] = res
        return res

    def back_to_product(u, c, up):
        gate = gate_ref[u, c]
        dres = (up * gate).astype(bf16)
        dres_ref[u, :, cells(c)] = dres
        dq_ref[u, 4 * C : 5 * C, cells(c)] = (up * res_ref[u, c] * gate * (1.0 - gate)).astype(bf16)
        return norm_back(dot(wo_ref[u], dres, 1, 0), ntri_ref[u, c], itri_ref[u, c])

    def back_to_factors(u, c, slot):
        mask = cell_mask(c)
        for g in range(2):
            d = big_recv[slot, g * 8 : (g + 1) * 8, c].reshape(C, W).astype(f32)
            sg = sg_ref[u, c, g * C : (g + 1) * C]
            dv = d * sg * mask
            dq_ref[u, g * C : (g + 1) * C, cells(c)] = dv.astype(bf16)
            dg = dv * v_ref[u, c, g * C : (g + 1) * C] * (1.0 - sg)
            dq_ref[u, (2 + g) * C : (3 + g) * C, cells(c)] = dg.astype(bf16)

    def back_to_pair(u, c):
        d = dot(wp_ref[u], dq_ref[u, :, cells(c)], 1, 0)
        return norm_back(d, n_ref[u, c], inv_ref[u, c])

    def halves(slot, p):
        x = small_recv[slot, :, p].astype(f32).reshape(D, 2, 8, W)
        return x[:, 0].reshape(C, W), x[:, 1].reshape(C, W)

    def put_halves(p, pieces):
        both = [y.reshape(D, 1, 8, W) for y in pieces]
        small_send[:, p] = jnp.concatenate(both, 1).reshape(D, 16, W).astype(bf16)

    def put_rows(ref, at, x):
        rows = ref.shape[1]
        x = x.astype(bf16)
        for k in range(x.shape[0] // 16):
            r = at + 16 * k
            ref[r // rows, r % rows : r % rows + 16] = x[16 * k : 16 * k + 16]

    def out_grad(u):
        return dot(xz_ref[u], dres_ref[u], 1, 1)

    def spread(x, row, step):
        a_ref[pl.ds(row, step)] = x[:, 0:C]
        a_ref[pl.ds(row + step, step)] = x[:, C : 2 * C]
        tail = x[:, 2 * C : W]
        b_ref[pl.ds(row, step)] = tail
        b_ref[pl.ds(row + step, step)] = pltpu.roll(tail, 64, 1)

    def collect(row, step):
        lane = lax.broadcasted_iota(jnp.int32, (step, C), 1)
        tail = jnp.where(lane < 64, b_ref[pl.ds(row, step)], b_ref[pl.ds(row + step, step)])
        return jnp.concatenate([a_ref[pl.ds(row, step)], a_ref[pl.ds(row + step, step)], tail], 1)

    def get_channel(ch, step):
        a = a_ref[pl.ds(ch, N, stride=step), :]
        b = b_ref[pl.ds(ch, N, stride=step), :]
        return a.astype(bf16), b[:, :64].astype(bf16)

    def put_channel(ch, step, x):
        a_ref[pl.ds(ch, N, stride=step), :] = x[:, 0:C]
        b_ref[pl.ds(ch, N, stride=step), :] = jnp.concatenate([x[:, C:N], x[:, C:N]], 1)

    def arrive(send, recv, phase, k):
        src = src_of(k)

        @pl.when(k == 0)
        def _():
            own_copy(send, recv, phase).wait()

        @pl.when(k > 0)
        def _():
            wait_from(send, recv, phase, src)

        return src

    def depart(send, recv, phase, k):
        peer = peer_of(k)

        @pl.when(k == 0)
        def _():
            own_copy(send, recv, phase).start()

        @pl.when(k > 0)
        def _():
            send_to(send, recv, phase, peer)

    def products(u, phase, slot):
        recv = big_recv.at[slot]

        @pl.loop(0, D)
        def _(k):
            src = arrive(big_send, recv, phase, k)
            for c in range(CH):
                spread(big_recv[slot, src, c].astype(f32), (src * R + 2 * c) * 16, 16)

        for ch in range(16):
            a, b = get_channel(ch, 16)
            lm_ref[u, ch, :, 0:C] = a
            lm_ref[u, ch, :, C:N] = b
        for ch in range(8):
            left, right = lm_ref[u, ch], lm_ref[u, 8 + ch]
            axis = 1 - u
            put_channel(ch, 8, dot(left, right, axis, axis))

        @pl.loop(0, D)
        def _(k):
            peer = peer_of(k)
            for p in range(CH // 2):
                row = (peer * R + 4 * p) * 8
                both = jnp.concatenate([collect(row, 8), collect(row + 16, 8)], 0)
                small_send[peer, p] = both.astype(bf16)
            depart(small_send, small_recv.at[slot], phase + 1, k)

    def product_grads(u, phase, slot):
        recv = small_recv.at[slot]

        @pl.loop(0, D)
        def _(k):
            src = arrive(small_send, recv, phase, k)
            for p in range(CH // 2):
                x = small_recv[slot, src, p].astype(f32)
                row = (src * R + 4 * p) * 8
                spread(x[0:8], row, 8)
                spread(x[8:16], row + 16, 8)

        for ch in range(8):
            a, b = get_channel(ch, 8)
            tm_ref[ch, :, 0:C] = a
            tm_ref[ch, :, C:N] = b
        for ch in range(8):
            left, right, grad = lm_ref[u, ch], lm_ref[u, 8 + ch], tm_ref[ch]
            if u == 0:
                dleft, dright = dot(grad, right, 1, 0), dot(grad, left, 0, 0)
            else:
                dleft, dright = dot(right, grad, 1, 1), dot(left, grad, 1, 0)
            put_channel(ch, 16, dleft)
            put_channel(8 + ch, 16, dright)

        @pl.loop(0, D)
        def _(k):
            peer = peer_of(k)
            for c in range(CH):
                big_send[peer, c] = collect((peer * R + 2 * c) * 16, 16).astype(bf16)
            depart(big_send, big_recv.at[slot], phase + 1, k)

    def start_sum(rows, arrived, phase):
        own_copy(rows, arrived, phase).start()

        @pl.loop(1, D)
        def _(k):
            send_to(rows, arrived, phase, peer_of(k))

    def mate_copy(src, dst, n):
        return pltpu.make_async_remote_copy(
            src_ref=src, dst_ref=dst, send_sem=core_s.at[n], recv_sem=core_r.at[n],
            device_id={"dp": mate}, device_id_type=MESH,
        )

    def z_copy(zbuf, n, peer, slot):
        return pltpu.make_async_remote_copy(
            src_ref=zbuf.at[slot], dst_ref=zbuf.at[slot],
            send_sem=zs.at[n, peer // 2], recv_sem=zr.at[n, slot],
            device_id={"dp": peer}, device_id_type=MESH,
        )

    def round_copy(everyone, phase, peer, slot):
        return pltpu.make_async_remote_copy(
            src_ref=everyone.at[slot], dst_ref=everyone.at[slot],
            send_sem=ssem.at[phase, peer], recv_sem=rsem.at[phase, slot],
            device_id={"dap": peer}, device_id_type=MESH,
        )

    def finish_sum(rows, arrived, phase, zbuf, everyone, n):
        half = rows.shape[1] // 2
        wait_all(rows, arrived, phase)

        def add(k, acc):
            return acc + arrived[k].astype(f32)

        total = lax.fori_loop(1, D, add, arrived[0].astype(f32))
        mine = jnp.where(core == 0, total[:half], total[half:])
        theirs = jnp.where(core == 0, total[half:], total[:half])
        half_out[n, 0:half] = theirs
        swap = mate_copy(half_out.at[n, pl.ds(0, half)], half_in.at[n, pl.ds(0, half)], n)
        swap.start()
        swap.wait_recv()
        zbuf[zed] = (mine + half_in[n, 0:half]).astype(bf16)

        @pl.loop(1, nz)
        def _(k):
            z_copy(zbuf, n, z_peer(k), zed).start()

        wait_sends(rows, arrived, phase)
        swap.wait_send()

        @pl.loop(1, nz)
        def _(k):
            peer = z_peer(nz - k)
            z_copy(zbuf, n, peer, peer // 2).wait_recv()

        def add_z(k, acc):
            return acc + zbuf[k].astype(f32)

        total = lax.fori_loop(1, nz, add_z, zbuf[0].astype(f32)).astype(bf16)
        mine = pl.ds(pl.multiple_of(core * half, half), half)
        everyone[me, mine] = total
        back = mate_copy(everyone.at[me, mine], everyone.at[me, mine], 2 + n)
        back.start()
        back.wait_recv()
        back.wait_send()

        @pl.loop(1, D)
        def _(k):
            round_copy(everyone, 10 + n, peer_of(k), me).start()

        @pl.loop(1, nz)
        def _(k):
            z_copy(zbuf, n, z_peer(k), zed).wait_send()

    def wait_round(everyone, phase):
        @pl.loop(1, D)
        def _(k):
            src = src_of(k)
            round_copy(everyone, phase, src, src).wait_recv()

        @pl.loop(1, D)
        def _(k):
            round_copy(everyone, phase, peer_of(k), me).wait_send()

    @pl.loop(0, CH)
    def _(c):
        project(0, c, load_cells(pair_ref, c))

    pl.semaphore_wait(barrier, D - 1 + nz)
    send_all(big_send, big_recv.at[0], 0)
    products(0, 0, 0)
    wait_sends(big_send, big_recv.at[0], 0)
    wait_all(small_send, small_recv.at[0], 1)

    @pl.loop(0, CH // 2)
    def _(p):
        for a, t in enumerate(halves(0, p)):
            c = 2 * p + a
            res = finish_product(0, c, t)
            one = (load_cells(pair_ref, c) + gate_ref[0, c] * res).astype(bf16)
            project(1, c, one.astype(f32))

    send_all(big_send, big_recv.at[1], 2)
    wait_sends(small_send, small_recv.at[0], 1)
    products(1, 2, 1)
    wait_sends(big_send, big_recv.at[1], 2)
    wait_all(small_send, small_recv.at[1], 3)
    wait_sends(small_send, small_recv.at[1], 3)

    @pl.loop(0, CH // 2)
    def _(p):
        pieces = []
        for a, t in enumerate(halves(1, p)):
            c = 2 * p + a
            finish_product(1, c, t)
            pieces.append(back_to_product(1, c, load_cells(cot_ref, c)))
        put_halves(p, pieces)

    send_all(small_send, small_recv.at[2], 4)
    put_rows(early, 5 * C, out_grad(1))
    product_grads(1, 4, 2)
    wait_sends(small_send, small_recv.at[2], 4)
    wait_all(big_send, big_recv.at[2], 5)

    @pl.loop(0, CH // 2)
    def _(p):
        pieces = []
        for a in range(2):
            c = 2 * p + a
            back_to_factors(1, c, 2)
            up = (load_cells(cot_ref, c) + back_to_pair(1, c)).astype(bf16)
            up_ref[c] = up
            pieces.append(back_to_product(0, c, up.astype(f32)))
        put_halves(p, pieces)

    send_all(small_send, small_recv.at[3], 6)
    wait_sends(big_send, big_recv.at[2], 5)
    put_rows(early, 0, dot(dq_ref[1], z_ref[1], 1, 1))
    put_rows(early, 6 * C, out_grad(0))
    put_rows(early, 7 * C, dot(dq_ref[0, 4 * C : 5 * C], z_ref[0], 1, 1))
    start_sum(early, early_in, 8)
    product_grads(0, 6, 3)
    wait_sends(small_send, small_recv.at[3], 6)
    finish_sum(early, early_in, 8, z_early, early_all, 0)
    wait_all(big_send, big_recv.at[3], 7)

    @pl.loop(0, CH)
    def _(c):
        back_to_factors(0, c, 3)

    put_rows(late, 0, dot(dq_ref[0, 0 : 4 * C], z_ref[0], 1, 1))
    start_sum(late, late_in, 9)

    @pl.loop(0, CH)
    def _(c):
        total = up_ref[c].astype(f32) + back_to_pair(0, c)
        y = jnp.transpose(total).astype(bf16)
        i = 2 * c
        out_ref[i, 0:C] = y[0:C]
        out_ref[i + 1, 0:C] = y[C : 2 * C]
        out_ref[i, C:N] = y[2 * C : 2 * C + 64]
        out_ref[i + 1, C:N] = y[2 * C + 64 : W]

    wait_sends(big_send, big_recv.at[3], 7)
    finish_sum(late, late_in, 9, z_late, late_all, 1)
    wait_round(early_all, 10)
    wait_round(late_all, 11)

    def factors(x):
        blocks = []
        for e in range(2):
            for t in range(2):
                part = x[t * 2 * C : (t + 1) * 2 * C].reshape(D, 2, 8, C)[:, e]
                blocks.append(jnp.transpose(part.reshape(C, C)))
        return blocks

    first = early_all[...].astype(f32).reshape(EARLY, C) * (1.0 / N)
    last = late_all[...].astype(f32).reshape(LATE, C) * (1.0 / N)
    for u, x, gate in ((0, last, first[7 * C : 8 * C]), (1, first[0 : 4 * C], first[4 * C : 5 * C])):
        for k, block in enumerate(factors(x) + [jnp.transpose(gate)]):
            gin_ref[u, :, k * C : (k + 1) * C] = block
    gout_ref[0] = first[6 * C : 7 * C]
    gout_ref[1] = first[5 * C : 6 * C]


def local(ndp, pair, pair_cot, residue_mask, w_in, w_out):
    vmem = pl.BlockSpec(memory_space=pltpu.VMEM)
    nz = ndp // 2
    scratch = [
        pltpu.VMEM((2, 5 * C, C), bf16),
        pltpu.VMEM((2, C, 5 * C), bf16),
        pltpu.VMEM((2, C, C), bf16),
        pltpu.VMEM((2, CH, C, W), f32),
        pltpu.VMEM((2, CH, 1, W), f32),
        pltpu.VMEM((2, C, CELLS), bf16),
        pltpu.VMEM((2, CH, 2 * C, W), f32),
        pltpu.VMEM((2, CH, 2 * C, W), f32),
        pltpu.VMEM((2, CH, C, W), f32),
        pltpu.VMEM((2, CH, C, W), f32),
        pltpu.VMEM((2, CH, C, W), f32),
        pltpu.VMEM((2, CH, 1, W), f32),
        pltpu.VMEM((2, C, CELLS), bf16),
        pltpu.VMEM((CH, C, W), bf16),
        pltpu.VMEM((2, C, CELLS), bf16),
        pltpu.VMEM((2, 5 * C, CELLS), bf16),
        pltpu.VMEM((2, 16, N, N), bf16),
        pltpu.VMEM((8, N, N), bf16),
        pltpu.VMEM((N * 16, C), f32),
        pltpu.VMEM((N * 16, C), f32),
        pltpu.VMEM((D, CH, 16, W), bf16),
        pltpu.VMEM((D, CH // 2, 16, W), bf16),
        pltpu.VMEM((4, D, CH, 16, W), bf16),
        pltpu.VMEM((4, D, CH // 2, 16, W), bf16),
        pltpu.VMEM((D, EARLY // D, C), bf16),
        pltpu.VMEM((D, LATE // D, C), bf16),
        pltpu.VMEM((D, EARLY // D, C), bf16),
        pltpu.VMEM((D, LATE // D, C), bf16),
        pltpu.VMEM((2, EARLY // D // 2, C), f32),
        pltpu.VMEM((2, EARLY // D // 2, C), f32),
        pltpu.VMEM((nz, EARLY // D // 2, C), bf16),
        pltpu.VMEM((nz, LATE // D // 2, C), bf16),
        pltpu.VMEM((D, EARLY // D, C), bf16),
        pltpu.VMEM((D, LATE // D, C), bf16),
        pltpu.SemaphoreType.DMA((12, D)),
        pltpu.SemaphoreType.DMA((12, D)),
        pltpu.SemaphoreType.DMA((12,)),
        pltpu.SemaphoreType.DMA((4,)),
        pltpu.SemaphoreType.DMA((4,)),
        pltpu.SemaphoreType.DMA((2, nz)),
        pltpu.SemaphoreType.DMA((2, nz)),
    ]
    grad, in_total, out_total = pl.pallas_call(
        functools.partial(kernel, ndp),
        out_shape=(
            jax.ShapeDtypeStruct((R, N, C), bf16),
            jax.ShapeDtypeStruct((2, C, 5 * C), f32),
            jax.ShapeDtypeStruct((2, C, C), f32),
        ),
        in_specs=[vmem] * 5,
        out_specs=(vmem, vmem, vmem),
        scratch_shapes=scratch,
        compiler_params=pltpu.CompilerParams(
            collective_id=0, has_side_effects=True, vmem_limit_bytes=60 * 1024 * 1024
        ),
    )(pair[0], pair_cot[0], residue_mask, w_in, w_out)
    return grad[None], in_total, out_total


def solution(mesh):
    return jax.shard_map(
        functools.partial(local, mesh.shape["dp"]),
        mesh=mesh,
        in_specs=(P("dp", "dap", None, None), P("dp", "dap", None, None), P("dp", None), P(), P()),
        out_specs=(P("dp", "dap", None, None), P(), P()),
        check_vma=False,
    )
```

time: 194 us -> 165 us (0.85)
  Pallas kernels: 184 us -> 160 us
  local copies, waits for them, and re-layouts: 8.13 us -> 3.66 us
    pallas_call x1, Pallas kernels: 184 us -> 160 us  [local(): pl.pallas_call(functools.partial(kernel, ndp), out_shape=(jax.ShapeDtypeS...]
    unnamed x11 -> x7, local copies, waits for them, and re-layouts: 5.41 us -> 3.66 us
where the time goes in v2:
time: 165 us
  Pallas kernels  160 us (97%)
  local copies, waits for them, and re-layouts  3.66 us (2%)
    pallas_call x1, Pallas kernels, local(): pl.pallas_call(functools.partial(kernel, ndp), out_shape=(jax.ShapeDtypeS...  160 us
    unnamed x7, local copies, waits for them, and re-layouts  3.66 us

profile of v2, /device:TPU:1, one launch (start us, length us, event | category | flops | bytes accessed | tf_op | source)
XLA Modules:
  0.0 164.8 jit_solution(1193714343675858568)
XLA Ops:
  0.6 160.5 %shard_map.76 = (bf16[12,192,128]{2,1,0:T(8,128)(2,1)}, f32[2,128,640]{2,1,0:T(8,128)}, f32[2,128,128]{2,1,0:T(8,128)}) custom-call(bf16[12,192,128]{2,1,0:T(8,128)(2,1)} %bitcast.4, bf16[12,192,128]{2,1,0:T(8,128)(2,1)} %bitcast.5, s32[1,192]{1,0:T(1,128)} %mask_ref.1, bf16[2,128,640]{2,1,0:T(8,128)(2,1)} %win_ref.1, bf16[2,128,128]{2,1,0:T(8,128)(2,1)} %wo_ref.1), custom_call_target="tpu_custom_call" | custom-call | tf_op jit(solution)/shard_map/pallas_call | solution.py:551
  161.1 0.0 copy-start
  161.1 2.0 %copy.11 = bf16[1,12,192,128]{3,2,1,0:T(8,128)(2,1)} copy(bf16[1,12,192,128]{3,2,1,0:T(8,128)(2,1)} %bitcast.3) | data formatting | bytes 1179648
  163.1 0.0 copy-done
  163.1 0.0 copy-start.1
  163.1 0.8 copy.12
  163.9 0.2 copy-done.1
  164.1 0.7 copy.13
Async XLA Ops:
  161.1 2.0 %copy-start = (f32[2,128,640]{2,1,0:T(8,128)S(1)}, f32[2,128,640]{2,1,0:T(8,128)}, u32[]{:S(2)}) copy-start(f32[2,128,640]{2,1,0:T(8,128)} %get-tuple-element.13) | copy-start | bytes 1966084
  163.1 1.0 copy-start.1

commit v3 on v2

v3 whole, which is shorter than its diff:
```python
import functools

import jax
import jax.numpy as jnp
from jax import lax
from jax.experimental import pallas as pl
from jax.experimental.pallas import tpu as pltpu
from jax.sharding import PartitionSpec as P

EPS = 1e-05
D = 16
R = 12
N = 192
C = 128
CH = 6
W = 2 * N
CELLS = R * N
EARLY = 8 * C
LATE = 4 * C
FAR = (10, 6, 9, 11, 14, 2, 8, 5, 7, 13, 15, 1, 4, 3, 12)
f32 = jnp.float32
bf16 = jnp.bfloat16
MESH = pl.DeviceIdType.MESH


def dot(a, b, ca, cb):
    return lax.dot_general(a, b, (((ca,), (cb,)), ((), ())), preferred_element_type=f32)


def normal_form(x):
    centred = x - jnp.mean(x, 0, keepdims=True)
    inv = lax.rsqrt(jnp.mean(centred * centred, 0, keepdims=True) + EPS)
    return centred * inv, inv


def norm_back(d, n, inv):
    return inv * (d - jnp.mean(d, 0, keepdims=True) - n * jnp.mean(d * n, 0, keepdims=True))


def kernel(
    ndp,
    pair_ref, cot_ref, mask_ref, win_ref, wo_ref,
    out_ref, gin_ref, gout_ref,
    wt_ref, wp_ref, wot_ref,
    n_ref, inv_ref, z_ref, v_ref, sg_ref, gate_ref, res_ref, ntri_ref, itri_ref, xz_ref,
    up_ref, dres_ref, dq_ref, lm_ref, tm_ref, a_ref, b_ref,
    big_send, small_send, big_recv, small_recv,
    early, late, early_in, late_in, half_mine, half_out, half_in, z_early, z_late, early_all, late_all,
    ssem, rsem, lsem, core_s, core_r, zs, zr, stagger,
):
    me = lax.axis_index("dap")
    my = lax.axis_index("dp")
    core, zed, nz = lax.rem(my, 2), my // 2, ndp // 2
    mate = my + 1 - 2 * core

    def offset(k, sign):
        j = k * 0
        for n, step in enumerate(FAR):
            j = jnp.where(k == n + 1, step, j)
        a, b = j // 4, lax.rem(j, 4)
        dx, dy = a + core * (b - a), b + core * (a - b)
        return lax.rem(me // 4 + 4 + sign * dx, 4) * 4 + lax.rem(lax.rem(me, 4) + 4 + sign * dy, 4)

    def peer_of(k):
        return offset(k, 1)

    def src_of(k):
        return offset(k, -1)

    def z_peer(k):
        return 2 * lax.rem(zed + k, nz) + core

    barrier = pltpu.get_barrier_semaphore()

    @pl.loop(1, D)
    def _(k):
        pl.semaphore_signal(barrier, inc=1, device_id={"dap": peer_of(k)}, device_id_type=MESH)

    pl.semaphore_signal(barrier, inc=1, device_id={"dp": mate}, device_id_type=MESH)

    @pl.loop(1, nz)
    def _(k):
        pl.semaphore_signal(barrier, inc=1, device_id={"dp": z_peer(k)}, device_id_type=MESH)

    for u in range(2):
        wt = jnp.transpose(win_ref[u].astype(f32))
        pieces = []
        for t in range(2):
            left, right = (wt[(2 * e + t) * C : (2 * e + t + 1) * C].reshape(D, 8, C) for e in range(2))
            for g in range(2):
                at = slice(4 * g, 4 * g + 4)
                pieces.append(jnp.concatenate([left[:, at], right[:, at]], 1).reshape(C, C))
        wt = jnp.concatenate(pieces + [wt[4 * C : 5 * C]], 0)
        wt_ref[u] = wt.astype(bf16)
        wp_ref[u] = jnp.transpose(wt).astype(bf16)
        wot_ref[u] = jnp.transpose(wo_ref[u].astype(f32)).astype(bf16)

    count = jnp.sum(mask_ref[...].astype(f32), 1, keepdims=True)

    def cell_mask(c):
        lane = lax.broadcasted_iota(jnp.int32, (1, W), 1)
        second = ((lane >= C) & (lane < 2 * C)) | (lane >= 2 * C + 64)
        k = jnp.where(lane < C, lane, jnp.where(lane < 2 * C + 64, lane - C, lane - N))
        k = jnp.where((lane >= C) & (lane < 2 * C), lane - C, k)
        row = me * R + 2 * c + second.astype(jnp.int32)
        return jnp.where((jnp.maximum(k, row).astype(f32) < count), 1.0, 0.0).astype(f32)

    def cells(c):
        return pl.ds(pl.multiple_of(c * W, C), W)

    def load_cells(ref, c):
        i = 2 * c
        x = jnp.concatenate(
            [ref[i, 0:C], ref[i + 1, 0:C], ref[i, C:N], ref[i + 1, C:N]], 0
        )
        return jnp.transpose(x.astype(f32))

    def copy_of(send, recv, phase, peer, slot, src):
        return pltpu.make_async_remote_copy(
            src_ref=send.at[peer],
            dst_ref=recv.at[slot],
            send_sem=ssem.at[phase, peer],
            recv_sem=rsem.at[phase, src],
            device_id={"dap": peer},
            device_id_type=MESH,
        )

    def send_to(send, recv, phase, peer):
        copy_of(send, recv, phase, peer, me, me).start()

    def own_copy(send, recv, phase):
        return pltpu.make_async_copy(send.at[me], recv.at[me], lsem.at[phase])

    def wait_from(send, recv, phase, src):
        copy_of(send, recv, phase, src, src, src).wait_recv()

    def send_all(send, recv, phase):
        own_copy(send, recv, phase).start()

        @pl.loop(1, D)
        def _(k):
            send_to(send, recv, phase, peer_of(k))

    def wait_sends(send, recv, phase):
        @pl.loop(1, D)
        def _(k):
            copy_of(send, recv, phase, peer_of(k), me, me).wait_send()

    def wait_all(send, recv, phase):
        own_copy(send, recv, phase).wait()

        @pl.loop(1, D)
        def _(k):
            wait_from(send, recv, phase, src_of(k))

    def normalize(u, c, x):
        n, inv = normal_form(x)
        n_ref[u, c] = n
        inv_ref[u, c] = inv
        z_ref[u, :, cells(c)] = n.astype(bf16)

    def factors_of(u, c, g):
        z = z_ref[u, :, cells(c)]
        v = dot(wt_ref[u, g * C : (g + 1) * C], z, 1, 0)
        sg = jax.nn.sigmoid(dot(wt_ref[u, (2 + g) * C : (3 + g) * C], z, 1, 0))
        v_ref[u, c, g * C : (g + 1) * C] = v
        sg_ref[u, c, g * C : (g + 1) * C] = sg
        return sg * v * cell_mask(c)

    def second_group(u):
        @pl.loop(0, CH // 2)
        def _(p):
            put_halves(big_send.at[1], p, [factors_of(u, 2 * p + a, 1) for a in range(2)])
            for a in range(2):
                c = 2 * p + a
                gate_ref[u, c] = jax.nn.sigmoid(dot(wt_ref[u, 4 * C : 5 * C], z_ref[u, :, cells(c)], 1, 0))

    def finish_product(u, c, t):
        n, inv = normal_form(t)
        ntri_ref[u, c] = n
        itri_ref[u, c] = inv
        xz = n.astype(bf16)
        xz_ref[u, :, cells(c)] = xz
        res = dot(wot_ref[u], xz, 1, 0)
        res_ref[u, c] = res
        return res

    def back_to_product(u, c, up):
        gate = gate_ref[u, c]
        dres = (up * gate).astype(bf16)
        dres_ref[u, :, cells(c)] = dres
        dq_ref[u, 4 * C : 5 * C, cells(c)] = (up * res_ref[u, c] * gate * (1.0 - gate)).astype(bf16)
        return norm_back(dot(wo_ref[u], dres, 1, 0), ntri_ref[u, c], itri_ref[u, c])

    def back_to_factors(u, p, g, slot):
        for a, d in enumerate(halves(big_recv.at[slot, g], p)):
            c = 2 * p + a
            sg = sg_ref[u, c, g * C : (g + 1) * C]
            dv = d * sg * cell_mask(c)
            dq_ref[u, g * C : (g + 1) * C, cells(c)] = dv.astype(bf16)
            dg = dv * v_ref[u, c, g * C : (g + 1) * C] * (1.0 - sg)
            dq_ref[u, (2 + g) * C : (3 + g) * C, cells(c)] = dg.astype(bf16)

    def back_to_pair(u, c):
        d = dot(wp_ref[u], dq_ref[u, :, cells(c)], 1, 0)
        return norm_back(d, n_ref[u, c], inv_ref[u, c])

    def halves(ref, p):
        x = ref[:, p].astype(f32).reshape(D, 2, 8, W)
        return x[:, 0].reshape(C, W), x[:, 1].reshape(C, W)

    def put_halves(ref, p, pieces):
        both = [y.reshape(D, 1, 8, W) for y in pieces]
        ref[:, p] = jnp.concatenate(both, 1).reshape(D, 16, W).astype(bf16)

    def put_rows(ref, at, x):
        rows = ref.shape[1]
        x = x.astype(bf16)
        for k in range(x.shape[0] // 16):
            r = at + 16 * k
            ref[r // rows, r % rows : r % rows + 16] = x[16 * k : 16 * k + 16]

    def out_grad(u):
        return dot(xz_ref[u], dres_ref[u], 1, 1)

    def spread(q, x, row):
        a_ref[q, pl.ds(row, 8)] = x[:, 0:C]
        a_ref[q, pl.ds(row + 8, 8)] = x[:, C : 2 * C]
        tail = x[:, 2 * C : W]
        b_ref[q, pl.ds(row, 8)] = tail
        b_ref[q, pl.ds(row + 8, 8)] = pltpu.roll(tail, 64, 1)

    def collect(q, row):
        lane = lax.broadcasted_iota(jnp.int32, (8, C), 1)
        tail = jnp.where(lane < 64, b_ref[q, pl.ds(row, 8)], b_ref[q, pl.ds(row + 8, 8)])
        return jnp.concatenate([a_ref[q, pl.ds(row, 8)], a_ref[q, pl.ds(row + 8, 8)], tail], 1)

    def get_channel(q, ch):
        a = a_ref[q, pl.ds(ch, N, stride=8), :]
        b = b_ref[q, pl.ds(ch, N, stride=8), :]
        return a.astype(bf16), b[:, :64].astype(bf16)

    def put_channel(q, ch, x):
        a_ref[q, pl.ds(ch, N, stride=8), :] = x[:, 0:C]
        b_ref[q, pl.ds(ch, N, stride=8), :] = jnp.concatenate([x[:, C:N], x[:, C:N]], 1)

    def arrive(send, recv, phase, k):
        src = src_of(k)

        @pl.when(k == 0)
        def _():
            own_copy(send, recv, phase).wait()

        @pl.when(k > 0)
        def _():
            wait_from(send, recv, phase, src)

        return src

    def depart(send, recv, phase, k):
        peer = peer_of(k)

        @pl.when(k == 0)
        def _():
            own_copy(send, recv, phase).start()

        @pl.when(k > 0)
        def _():
            send_to(send, recv, phase, peer)

    def unpack(q, send, recv, phase):
        @pl.loop(0, D)
        def _(k):
            src = arrive(send, recv, phase, k)
            for p in range(CH // 2):
                x = recv[src, p].astype(f32)
                row = (src * R + 4 * p) * 8
                spread(q, x[0:8], row)
                spread(q, x[8:16], row + 16)

    def pack(q, send, recv, phase):
        @pl.loop(0, D)
        def _(k):
            peer = peer_of(k)
            for p in range(CH // 2):
                row = (peer * R + 4 * p) * 8
                send[peer, p] = jnp.concatenate([collect(q, row), collect(q, row + 16)], 0).astype(bf16)
            depart(send, recv, phase, k)

    def products(u, phase, slot):
        for g in range(2):
            unpack(g, big_send.at[g], big_recv.at[slot, g], phase + g)
            for ch in range(8):
                a, b = get_channel(g, ch)
                lm_ref[u, g, ch, :, 0:C] = a
                lm_ref[u, g, ch, :, C:N] = b
            for e in range(4):
                axis = 1 - u
                put_channel(2, 4 * g + e, dot(lm_ref[u, g, e], lm_ref[u, g, 4 + e], axis, axis))
        pack(2, small_send, small_recv.at[slot], phase + 2)

    def product_grads(u, phase, slot):
        unpack(2, small_send, small_recv.at[slot], phase)
        for ch in range(8):
            a, b = get_channel(2, ch)
            tm_ref[ch, :, 0:C] = a
            tm_ref[ch, :, C:N] = b
        for g in range(2):
            for e in range(4):
                left, right, grad = lm_ref[u, g, e], lm_ref[u, g, 4 + e], tm_ref[4 * g + e]
                if u == 0:
                    dleft, dright = dot(grad, right, 1, 0), dot(grad, left, 0, 0)
                else:
                    dleft, dright = dot(right, grad, 1, 1), dot(left, grad, 1, 0)
                put_channel(g, e, dleft)
                put_channel(g, 4 + e, dright)
            pack(g, big_send.at[g], big_recv.at[slot, g], phase + 1 + g)

    def start_sum(rows, arrived, phase):
        own_copy(rows, arrived, phase).start()

        @pl.loop(1, D)
        def _(k):
            send_to(rows, arrived, phase, peer_of(k))

    def mate_copy(src, dst, n):
        return pltpu.make_async_remote_copy(
            src_ref=src, dst_ref=dst, send_sem=core_s.at[n], recv_sem=core_r.at[n],
            device_id={"dp": mate}, device_id_type=MESH,
        )

    def z_copy(zbuf, n, peer, slot):
        return pltpu.make_async_remote_copy(
            src_ref=zbuf.at[slot], dst_ref=zbuf.at[slot],
            send_sem=zs.at[n, peer // 2], recv_sem=zr.at[n, slot],
            device_id={"dp": peer}, device_id_type=MESH,
        )

    def round_copy(everyone, phase, peer, slot):
        return pltpu.make_async_remote_copy(
            src_ref=everyone.at[slot], dst_ref=everyone.at[slot],
            send_sem=ssem.at[phase, peer], recv_sem=rsem.at[phase, slot],
            device_id={"dap": peer}, device_id_type=MESH,
        )

    def own_half(rows):
        half = rows.shape[1] // 2
        return pl.ds(pl.multiple_of(core * half, half), half)

    def swap_halves(rows, n):
        half = rows.shape[1] // 2
        return mate_copy(half_out.at[n, pl.ds(0, half)], half_in.at[n, pl.ds(0, half)], n)

    def sum_over_dap(rows, arrived, phase, n):
        half = rows.shape[1] // 2
        wait_all(rows, arrived, phase)

        def add(k, acc):
            return acc + arrived[k].astype(f32)

        total = lax.fori_loop(1, D, add, arrived[0].astype(f32))
        half_mine[n, 0:half] = jnp.where(core == 0, total[:half], total[half:])
        half_out[n, 0:half] = jnp.where(core == 0, total[half:], total[:half])
        swap_halves(rows, n).start()

    def send_along_z(rows, zbuf, n):
        half = rows.shape[1] // 2
        swap_halves(rows, n).wait_recv()
        zbuf[zed] = (half_mine[n, 0:half] + half_in[n, 0:half]).astype(bf16)

        @pl.loop(1, nz)
        def _(k):
            z_copy(zbuf, n, z_peer(k), zed).start()

    def hand_round(rows, zbuf, everyone, phase, n):
        @pl.loop(1, nz)
        def _(k):
            peer = z_peer(nz - k)
            z_copy(zbuf, n, peer, peer // 2).wait_recv()

        def add(k, acc):
            return acc + zbuf[k].astype(f32)

        total = lax.fori_loop(1, nz, add, zbuf[0].astype(f32)).astype(bf16)
        mine = own_half(rows)
        everyone[me, mine] = total
        back = mate_copy(everyone.at[me, mine], everyone.at[me, mine], 2 + n)
        back.start()
        back.wait_recv()

        @pl.loop(1, D)
        def _(k):
            round_copy(everyone, phase, peer_of(k), me).start()

    def end_sum(rows, arrived, phase, zbuf, everyone, n):
        wait_sends(rows, arrived, phase)
        swap_halves(rows, n).wait_send()
        mate_copy(everyone.at[me, own_half(rows)], everyone.at[me, own_half(rows)], 2 + n).wait_send()

        @pl.loop(1, nz)
        def _(k):
            z_copy(zbuf, n, z_peer(k), zed).wait_send()

    def wait_round(everyone, phase):
        @pl.loop(1, D)
        def _(k):
            src = src_of(k)
            round_copy(everyone, phase, src, src).wait_recv()

        @pl.loop(1, D)
        def _(k):
            round_copy(everyone, phase, peer_of(k), me).wait_send()

    def big(slot, g):
        return big_send.at[g], big_recv.at[slot, g]

    def small(slot):
        return small_send, small_recv.at[slot]

    @pl.loop(0, CH // 2)
    def _(p):
        pieces = []
        for a in range(2):
            c = 2 * p + a
            normalize(0, c, load_cells(pair_ref, c))
            pieces.append(factors_of(0, c, 0))
        put_halves(big_send.at[0], p, pieces)

    pl.semaphore_wait(barrier, D - 1 + nz)

    @pl.when(core == 1)
    def _():
        pl.semaphore_wait(stagger, 1)

    send_all(*big(0, 0), 0)
    second_group(0)
    send_all(*big(0, 1), 1)
    wait_sends(*big(0, 0), 0)
    wait_sends(*big(0, 1), 1)

    @pl.when(core == 0)
    def _():
        pl.semaphore_signal(stagger, inc=1, device_id={"dp": mate}, device_id_type=MESH)

    products(0, 0, 0)
    wait_all(*small(0), 2)

    @pl.loop(0, CH // 2)
    def _(p):
        pieces = []
        for a, t in enumerate(halves(small_recv.at[0], p)):
            c = 2 * p + a
            res = finish_product(0, c, t)
            one = (load_cells(pair_ref, c) + gate_ref[0, c] * res).astype(bf16)
            normalize(1, c, one.astype(f32))
            pieces.append(factors_of(1, c, 0))
        put_halves(big_send.at[0], p, pieces)

    send_all(*big(1, 0), 3)
    second_group(1)
    send_all(*big(1, 1), 4)
    wait_sends(*small(0), 2)
    products(1, 3, 1)
    wait_sends(*big(1, 0), 3)
    wait_sends(*big(1, 1), 4)
    wait_all(*small(1), 5)
    wait_sends(*small(1), 5)

    @pl.loop(0, CH // 2)
    def _(p):
        pieces = []
        for a, t in enumerate(halves(small_recv.at[1], p)):
            c = 2 * p + a
            finish_product(1, c, t)
            pieces.append(back_to_product(1, c, load_cells(cot_ref, c)))
        put_halves(small_send, p, pieces)

    send_all(*small(2), 6)
    put_rows(early, 5 * C, out_grad(1))
    product_grads(1, 6, 2)
    wait_sends(*small(2), 6)
    wait_all(*big(2, 0), 7)

    @pl.loop(0, CH // 2)
    def _(p):
        back_to_factors(1, p, 0, 2)

    wait_all(*big(2, 1), 8)

    @pl.loop(0, CH // 2)
    def _(p):
        back_to_factors(1, p, 1, 2)
        pieces = []
        for a in range(2):
            c = 2 * p + a
            up = (load_cells(cot_ref, c) + back_to_pair(1, c)).astype(bf16)
            up_ref[c] = up
            pieces.append(back_to_product(0, c, up.astype(f32)))
        put_halves(small_send, p, pieces)

    send_all(*small(3), 9)
    put_rows(early, 0, dot(dq_ref[1], z_ref[1], 1, 1))
    put_rows(early, 6 * C, out_grad(0))
    put_rows(early, 7 * C, dot(dq_ref[0, 4 * C : 5 * C], z_ref[0], 1, 1))
    start_sum(early, early_in, 12)
    wait_sends(*big(2, 0), 7)
    wait_sends(*big(2, 1), 8)
    product_grads(0, 9, 3)
    wait_sends(*small(3), 9)
    sum_over_dap(early, early_in, 12, 0)
    wait_all(*big(3, 0), 10)

    @pl.loop(0, CH // 2)
    def _(p):
        back_to_factors(0, p, 0, 3)

    send_along_z(early, z_early, 0)
    wait_all(*big(3, 1), 11)

    @pl.loop(0, CH // 2)
    def _(p):
        back_to_factors(0, p, 1, 3)

    put_rows(late, 0, dot(dq_ref[0, 0 : 4 * C], z_ref[0], 1, 1))
    start_sum(late, late_in, 13)

    @pl.loop(0, CH)
    def _(c):
        total = up_ref[c].astype(f32) + back_to_pair(0, c)
        y = jnp.transpose(total).astype(bf16)
        i = 2 * c
        out_ref[i, 0:C] = y[0:C]
        out_ref[i + 1, 0:C] = y[C : 2 * C]
        out_ref[i, C:N] = y[2 * C : 2 * C + 64]
        out_ref[i + 1, C:N] = y[2 * C + 64 : W]

    wait_sends(*big(3, 0), 10)
    wait_sends(*big(3, 1), 11)
    sum_over_dap(late, late_in, 13, 1)
    send_along_z(late, z_late, 1)
    hand_round(early, z_early, early_all, 14, 0)
    hand_round(late, z_late, late_all, 15, 1)
    wait_round(early_all, 14)
    wait_round(late_all, 15)
    end_sum(early, early_in, 12, z_early, early_all, 0)
    end_sum(late, late_in, 13, z_late, late_all, 1)

    def factors(x):
        blocks = []
        for e in range(2):
            for t in range(2):
                groups = [x[(2 * t + g) * C : (2 * t + g + 1) * C].reshape(D, 8, C) for g in range(2)]
                part = jnp.concatenate([y[:, 4 * e : 4 * e + 4] for y in groups], 1)
                blocks.append(jnp.transpose(part.reshape(C, C)))
        return blocks

    first = early_all[...].astype(f32).reshape(EARLY, C) * (1.0 / N)
    last = late_all[...].astype(f32).reshape(LATE, C) * (1.0 / N)
    for u, x, gate in ((0, last, first[7 * C : 8 * C]), (1, first[0 : 4 * C], first[4 * C : 5 * C])):
        for k, block in enumerate(factors(x) + [jnp.transpose(gate)]):
            gin_ref[u, :, k * C : (k + 1) * C] = block
    gout_ref[0] = first[6 * C : 7 * C]
    gout_ref[1] = first[5 * C : 6 * C]


def hand_over(a, b, c, x, y, z, sems):
    copies = [pltpu.make_async_copy(s, t, sems.at[k]) for k, (s, t) in enumerate(((a, x), (b, y), (c, z)))]
    for copy in copies:
        copy.start()
    for copy in copies:
        copy.wait()


def local(ndp, pair, pair_cot, residue_mask, w_in, w_out):
    vmem = pl.BlockSpec(memory_space=pltpu.VMEM)
    nz = ndp // 2
    scratch = [
        pltpu.VMEM((2, 5 * C, C), bf16),
        pltpu.VMEM((2, C, 5 * C), bf16),
        pltpu.VMEM((2, C, C), bf16),
        pltpu.VMEM((2, CH, C, W), f32),
        pltpu.VMEM((2, CH, 1, W), f32),
        pltpu.VMEM((2, C, CELLS), bf16),
        pltpu.VMEM((2, CH, 2 * C, W), f32),
        pltpu.VMEM((2, CH, 2 * C, W), f32),
        pltpu.VMEM((2, CH, C, W), f32),
        pltpu.VMEM((2, CH, C, W), f32),
        pltpu.VMEM((2, CH, C, W), f32),
        pltpu.VMEM((2, CH, 1, W), f32),
        pltpu.VMEM((2, C, CELLS), bf16),
        pltpu.VMEM((CH, C, W), bf16),
        pltpu.VMEM((2, C, CELLS), bf16),
        pltpu.VMEM((2, 5 * C, CELLS), bf16),
        pltpu.VMEM((2, 2, 8, N, N), bf16),
        pltpu.VMEM((8, N, N), bf16),
        pltpu.VMEM((3, N * 8, C), f32),
        pltpu.VMEM((3, N * 8, C), f32),
        pltpu.VMEM((2, D, CH // 2, 16, W), bf16),
        pltpu.VMEM((D, CH // 2, 16, W), bf16),
        pltpu.VMEM((4, 2, D, CH // 2, 16, W), bf16),
        pltpu.VMEM((4, D, CH // 2, 16, W), bf16),
        pltpu.VMEM((D, EARLY // D, C), bf16),
        pltpu.VMEM((D, LATE // D, C), bf16),
        pltpu.VMEM((D, EARLY // D, C), bf16),
        pltpu.VMEM((D, LATE // D, C), bf16),
        pltpu.VMEM((2, EARLY // D // 2, C), f32),
        pltpu.VMEM((2, EARLY // D // 2, C), f32),
        pltpu.VMEM((2, EARLY // D // 2, C), f32),
        pltpu.VMEM((nz, EARLY // D // 2, C), bf16),
        pltpu.VMEM((nz, LATE // D // 2, C), bf16),
        pltpu.VMEM((D, EARLY // D, C), bf16),
        pltpu.VMEM((D, LATE // D, C), bf16),
        pltpu.SemaphoreType.DMA((16, D)),
        pltpu.SemaphoreType.DMA((16, D)),
        pltpu.SemaphoreType.DMA((16,)),
        pltpu.SemaphoreType.DMA((4,)),
        pltpu.SemaphoreType.DMA((4,)),
        pltpu.SemaphoreType.DMA((2, nz)),
        pltpu.SemaphoreType.DMA((2, nz)),
        pltpu.SemaphoreType.REGULAR,
    ]
    grad, in_total, out_total = pl.pallas_call(
        functools.partial(kernel, ndp),
        out_shape=(
            jax.ShapeDtypeStruct((R, N, C), bf16),
            jax.ShapeDtypeStruct((2, C, 5 * C), f32),
            jax.ShapeDtypeStruct((2, C, C), f32),
        ),
        in_specs=[vmem] * 5,
        out_specs=(vmem, vmem, vmem),
        scratch_shapes=scratch,
        compiler_params=pltpu.CompilerParams(
            collective_id=0, has_side_effects=True, vmem_limit_bytes=60 * 1024 * 1024
        ),
    )(pair[0], pair_cot[0], residue_mask, w_in, w_out)
    results = (grad, in_total, out_total)
    anywhere = pl.BlockSpec(memory_space=pltpu.HBM)
    grad, in_total, out_total = pl.pallas_call(
        hand_over,
        out_shape=tuple(jax.ShapeDtypeStruct(x.shape, x.dtype) for x in results),
        in_specs=[vmem] * 3,
        out_specs=(anywhere,) * 3,
        scratch_shapes=[pltpu.SemaphoreType.DMA((3,))],
    )(*results)
    return grad[None], in_total, out_total


def solution(mesh):
    return jax.shard_map(
        functools.partial(local, mesh.shape["dp"]),
        mesh=mesh,
        in_specs=(P("dp", "dap", None, None), P("dp", "dap", None, None), P("dp", None), P(), P()),
        out_specs=(P("dp", "dap", None, None), P(), P()),
        check_vma=False,
    )
```

time: 165 us -> 151 us (0.915)
  Pallas kernels: 160 us -> 150 us
  local copies, waits for them, and re-layouts: 3.66 us -> 0 us
    pallas_call x1, Pallas kernels: 160 us -> 148 us  [local(): pl.pallas_call(functools.partial(kernel, ndp), out_shape=(jax.ShapeDtypeS...]
    unnamed x7 -> x0, local copies, waits for them, and re-layouts: 3.66 us -> none
    pallas_call x0 -> x1, Pallas kernels: none -> 2.37 us  [local(): pl.pallas_call(hand_over, out_shape=tuple((jax.ShapeDtypeStruct(x.shape,...]
where the time goes in v3:
time: 151 us
  Pallas kernels  150 us (99%)
    pallas_call x1, Pallas kernels, local(): pl.pallas_call(functools.partial(kernel, ndp), out_shape=(jax.ShapeDtypeS...  148 us

profile of v3, /device:TPU:1, one launch (start us, length us, event | category | flops | bytes accessed | tf_op | source)
XLA Modules:
  0.0 150.7 jit_solution(8103303522847076639)
XLA Ops:
  0.6 147.7 %shard_map.76 = (bf16[12,192,128]{2,1,0:T(8,128)(2,1)}, f32[2,128,640]{2,1,0:T(8,128)}, f32[2,128,128]{2,1,0:T(8,128)}) custom-call(bf16[12,192,128]{2,1,0:T(8,128)(2,1)} %bitcast.3, bf16[12,192,128]{2,1,0:T(8,128)(2,1)} %bitcast.4, s32[1,192]{1,0:T(1,128)} %mask_ref.1, bf16[2,128,640]{2,1,0:T(8,128)(2,1)} %win_ref.1, bf16[2,128,128]{2,1,0:T(8,128)(2,1)} %wo_ref.1), custom_call_target="tpu_custom_call" | custom-call | tf_op jit(solution)/shard_map/pallas_call | solution.py:622
  148.3 2.4 %shard_map.77 = (bf16[12,192,128]{2,1,0:T(8,128)(2,1)}, f32[2,128,640]{2,1,0:T(8,128)}, f32[2,128,128]{2,1,0:T(8,128)}) custom-call(bf16[12,192,128]{2,1,0:T(8,128)(2,1)} %get-tuple-element.9.a, f32[2,128,640]{2,1,0:T(8,128)} %get-tuple-element.10.b, f32[2,128,128]{2,1,0:T(8,128)} %get-tuple-element.11.c), custom_call_target="tpu_custom_call" | custom-call | tf_op jit(solution)/shard_map/pallas_call | solution.py:638

commit v4 on v3

--- a/solution.py
+++ b/solution.py
@@ -27,6 +27,10 @@
     return lax.dot_general(a, b, (((ca,), (cb,)), ((), ())), preferred_element_type=f32)
 
 
+def sigmoid(x):
+    return 0.5 * jnp.tanh(0.5 * x) + 0.5
+
+
 def normal_form(x):
     centred = x - jnp.mean(x, 0, keepdims=True)
     inv = lax.rsqrt(jnp.mean(centred * centred, 0, keepdims=True) + EPS)
@@ -43,10 +47,10 @@
     out_ref, gin_ref, gout_ref,
     wt_ref, wp_ref, wot_ref,
     n_ref, inv_ref, z_ref, v_ref, sg_ref, gate_ref, res_ref, ntri_ref, itri_ref, xz_ref,
-    up_ref, dres_ref, dq_ref, lm_ref, tm_ref, a_ref, b_ref,
+    pt_ref, ct_ref, up_ref, dres_ref, dq_ref, lm_ref, tm_ref, a_ref, b_ref,
     big_send, small_send, big_recv, small_recv,
     early, late, early_in, late_in, half_mine, half_out, half_in, z_early, z_late, early_all, late_all,
-    ssem, rsem, lsem, core_s, core_r, zs, zr, stagger,
+    ssem, rsem, lsem, gs, gr, own, core_s, core_r, zs, zr,
 ):
     me = lax.axis_index("dap")
     my = lax.axis_index("dp")
@@ -115,43 +119,38 @@
         )
         return jnp.transpose(x.astype(f32))
 
-    def copy_of(send, recv, phase, peer, slot, src):
+    def part_copy(send, recv, phase, p, peer, slot):
         return pltpu.make_async_remote_copy(
-            src_ref=send.at[peer],
-            dst_ref=recv.at[slot],
-            send_sem=ssem.at[phase, peer],
-            recv_sem=rsem.at[phase, src],
-            device_id={"dap": peer},
-            device_id_type=MESH,
+            src_ref=send.at[p, peer], dst_ref=recv.at[p, slot],
+            send_sem=ssem.at[phase, p], recv_sem=rsem.at[phase, p],
+            device_id={"dap": peer}, device_id_type=MESH,
         )
 
-    def send_to(send, recv, phase, peer):
-        copy_of(send, recv, phase, peer, me, me).start()
-
-    def own_copy(send, recv, phase):
-        return pltpu.make_async_copy(send.at[me], recv.at[me], lsem.at[phase])
-
-    def wait_from(send, recv, phase, src):
-        copy_of(send, recv, phase, src, src, src).wait_recv()
-
-    def send_all(send, recv, phase):
-        own_copy(send, recv, phase).start()
+    def own_copy(send, recv, phase, p):
+        return pltpu.make_async_copy(send.at[p, me], recv.at[p, me], lsem.at[phase, p])
+
+    def others(send, recv, phase, p):
+        rest = pl.ds(0, D - 1)
+        return pltpu.make_async_remote_copy(
+            src_ref=send.at[p, rest], dst_ref=recv.at[p, rest],
+            send_sem=ssem.at[phase, p], recv_sem=rsem.at[phase, p],
+            device_id={"dap": peer_of(1)}, device_id_type=MESH,
+        )
+
+    def send_part(send, recv, phase, p):
+        own_copy(send, recv, phase, p).start()
 
         @pl.loop(1, D)
         def _(k):
-            send_to(send, recv, phase, peer_of(k))
+            part_copy(send, recv, phase, p, peer_of(k), me).start()
+
+    def wait_part(send, recv, phase, p):
+        own_copy(send, recv, phase, p).wait()
+        others(send, recv, phase, p).wait_recv()
 
     def wait_sends(send, recv, phase):
-        @pl.loop(1, D)
-        def _(k):
-            copy_of(send, recv, phase, peer_of(k), me, me).wait_send()
-
-    def wait_all(send, recv, phase):
-        own_copy(send, recv, phase).wait()
-
-        @pl.loop(1, D)
-        def _(k):
-            wait_from(send, recv, phase, src_of(k))
+        for p in range(CH // 2):
+            others(send, recv, phase, p).wait_send()
 
     def normalize(u, c, x):
         n, inv = normal_form(x)
@@ -162,18 +161,19 @@
     def factors_of(u, c, g):
         z = z_ref[u, :, cells(c)]
         v = dot(wt_ref[u, g * C : (g + 1) * C], z, 1, 0)
-        sg = jax.nn.sigmoid(dot(wt_ref[u, (2 + g) * C : (3 + g) * C], z, 1, 0))
+        sg = sigmoid(dot(wt_ref[u, (2 + g) * C : (3 + g) * C], z, 1, 0))
         v_ref[u, c, g * C : (g + 1) * C] = v
         sg_ref[u, c, g * C : (g + 1) * C] = sg
         return sg * v * cell_mask(c)
 
-    def second_group(u):
+    def second_group(u, send, recv, phase):
         @pl.loop(0, CH // 2)
         def _(p):
-            put_halves(big_send.at[1], p, [factors_of(u, 2 * p + a, 1) for a in range(2)])
+            put_halves(send, p, [factors_of(u, 2 * p + a, 1) for a in range(2)])
+            send_part(send, recv, phase, p)
             for a in range(2):
                 c = 2 * p + a
-                gate_ref[u, c] = jax.nn.sigmoid(dot(wt_ref[u, 4 * C : 5 * C], z_ref[u, :, cells(c)], 1, 0))
+                gate_ref[u, c] = sigmoid(dot(wt_ref[u, 4 * C : 5 * C], z_ref[u, :, cells(c)], 1, 0))
 
     def finish_product(u, c, t):
         n, inv = normal_form(t)
@@ -206,12 +206,12 @@
         return norm_back(d, n_ref[u, c], inv_ref[u, c])
 
     def halves(ref, p):
-        x = ref[:, p].astype(f32).reshape(D, 2, 8, W)
+        x = ref[p].astype(f32).reshape(D, 2, 8, W)
         return x[:, 0].reshape(C, W), x[:, 1].reshape(C, W)
 
     def put_halves(ref, p, pieces):
         both = [y.reshape(D, 1, 8, W) for y in pieces]
-        ref[:, p] = jnp.concatenate(both, 1).reshape(D, 16, W).astype(bf16)
+        ref[p] = jnp.concatenate(both, 1).reshape(D, 16, W).astype(bf16)
 
     def put_rows(ref, at, x):
         rows = ref.shape[1]
@@ -244,48 +244,26 @@
         a_ref[q, pl.ds(ch, N, stride=8), :] = x[:, 0:C]
         b_ref[q, pl.ds(ch, N, stride=8), :] = jnp.concatenate([x[:, C:N], x[:, C:N]], 1)
 
-    def arrive(send, recv, phase, k):
-        src = src_of(k)
-
-        @pl.when(k == 0)
-        def _():
-            own_copy(send, recv, phase).wait()
-
-        @pl.when(k > 0)
-        def _():
-            wait_from(send, recv, phase, src)
-
-        return src
-
-    def depart(send, recv, phase, k):
-        peer = peer_of(k)
-
-        @pl.when(k == 0)
-        def _():
-            own_copy(send, recv, phase).start()
-
-        @pl.when(k > 0)
-        def _():
-            send_to(send, recv, phase, peer)
-
     def unpack(q, send, recv, phase):
-        @pl.loop(0, D)
-        def _(k):
-            src = arrive(send, recv, phase, k)
-            for p in range(CH // 2):
-                x = recv[src, p].astype(f32)
-                row = (src * R + 4 * p) * 8
+        for p in range(CH // 2):
+            wait_part(send, recv, phase, p)
+
+            @pl.loop(0, D)
+            def _(k):
+                x = recv[p, k].astype(f32)
+                row = (k * R + 4 * p) * 8
                 spread(q, x[0:8], row)
                 spread(q, x[8:16], row + 16)
 
     def pack(q, send, recv, phase):
-        @pl.loop(0, D)
-        def _(k):
-            peer = peer_of(k)
-            for p in range(CH // 2):
-                row = (peer * R + 4 * p) * 8
-                send[peer, p] = jnp.concatenate([collect(q, row), collect(q, row + 16)], 0).astype(bf16)
-            depart(send, recv, phase, k)
+        @pl.loop(0, CH // 2)
+        def _(p):
+            @pl.loop(0, D)
+            def _(k):
+                row = (k * R + 4 * p) * 8
+                send[p, k] = jnp.concatenate([collect(q, row), collect(q, row + 16)], 0).astype(bf16)
+
+            send_part(send, recv, phase, p)
 
     def products(u, phase, slot):
         for g in range(2):
@@ -316,12 +294,21 @@
                 put_channel(g, 4 + e, dright)
             pack(g, big_send.at[g], big_recv.at[slot, g], phase + 1 + g)
 
-    def start_sum(rows, arrived, phase):
-        own_copy(rows, arrived, phase).start()
+    def sum_copy(rows, arrived, n, peer, slot, dev=None):
+        return pltpu.make_async_remote_copy(
+            src_ref=rows.at[peer], dst_ref=arrived.at[slot], send_sem=gs.at[n], recv_sem=gr.at[n],
+            device_id={"dap": peer if dev is None else dev}, device_id_type=MESH,
+        )
+
+    def own_rows(rows, arrived, n):
+        return pltpu.make_async_copy(rows.at[me], arrived.at[me], own.at[n])
+
+    def start_sum(rows, arrived, n):
+        own_rows(rows, arrived, n).start()
 
         @pl.loop(1, D)
         def _(k):
-            send_to(rows, arrived, phase, peer_of(k))
+            sum_copy(rows, arrived, n, peer_of(k), me).start()
 
     def mate_copy(src, dst, n):
         return pltpu.make_async_remote_copy(
@@ -332,16 +319,19 @@
     def z_copy(zbuf, n, peer, slot):
         return pltpu.make_async_remote_copy(
             src_ref=zbuf.at[slot], dst_ref=zbuf.at[slot],
-            send_sem=zs.at[n, peer // 2], recv_sem=zr.at[n, slot],
+            send_sem=zs.at[n], recv_sem=zr.at[n],
             device_id={"dp": peer}, device_id_type=MESH,
         )
 
-    def round_copy(everyone, phase, peer, slot):
+    def round_copy(everyone, n, peer, slot):
         return pltpu.make_async_remote_copy(
             src_ref=everyone.at[slot], dst_ref=everyone.at[slot],
-            send_sem=ssem.at[phase, peer], recv_sem=rsem.at[phase, slot],
+            send_sem=gs.at[2 + n], recv_sem=gr.at[2 + n],
             device_id={"dap": peer}, device_id_type=MESH,
         )
+
+    rest = pl.ds(0, D - 1)
+    rest_z = pl.ds(0, nz - 1)
 
     def own_half(rows):
         half = rows.shape[1] // 2
@@ -351,9 +341,10 @@
         half = rows.shape[1] // 2
         return mate_copy(half_out.at[n, pl.ds(0, half)], half_in.at[n, pl.ds(0, half)], n)
 
-    def sum_over_dap(rows, arrived, phase, n):
+    def sum_over_dap(rows, arrived, n):
         half = rows.shape[1] // 2
-        wait_all(rows, arrived, phase)
+        own_rows(rows, arrived, n).wait()
+        sum_copy(rows, arrived, n, rest, rest, peer_of(1)).wait_recv()
 
         def add(k, acc):
             return acc + arrived[k].astype(f32)
@@ -372,11 +363,9 @@
         def _(k):
             z_copy(zbuf, n, z_peer(k), zed).start()
 
-    def hand_round(rows, zbuf, everyone, phase, n):
-        @pl.loop(1, nz)
-        def _(k):
-            peer = z_peer(nz - k)
-            z_copy(zbuf, n, peer, peer // 2).wait_recv()
+    def hand_round(rows, zbuf, everyone, n):
+        if nz > 1:
+            z_copy(zbuf, n, z_peer(1), rest_z).wait_recv()
 
         def add(k, acc):
             return acc + zbuf[k].astype(f32)
@@ -390,26 +379,15 @@
 
         @pl.loop(1, D)
         def _(k):
-            round_copy(everyone, phase, peer_of(k), me).start()
-
-    def end_sum(rows, arrived, phase, zbuf, everyone, n):
-        wait_sends(rows, arrived, phase)
+            round_copy(everyone, n, peer_of(k), me).start()
+
+    def end_sum(rows, arrived, zbuf, everyone, n):
+        sum_copy(rows, arrived, n, rest, rest, peer_of(1)).wait_send()
+        round_copy(everyone, n, peer_of(1), rest).wait_send()
         swap_halves(rows, n).wait_send()
         mate_copy(everyone.at[me, own_half(rows)], everyone.at[me, own_half(rows)], 2 + n).wait_send()
-
-        @pl.loop(1, nz)
-        def _(k):
-            z_copy(zbuf, n, z_peer(k), zed).wait_send()
-
-    def wait_round(everyone, phase):
-        @pl.loop(1, D)
-        def _(k):
-            src = src_of(k)
-            round_copy(everyone, phase, src, src).wait_recv()
-
-        @pl.loop(1, D)
-        def _(k):
-            round_copy(everyone, phase, peer_of(k), me).wait_send()
+        if nz > 1:
+            z_copy(zbuf, n, z_peer(1), rest_z).wait_send()
 
     def big(slot, g):
         return big_send.at[g], big_recv.at[slot, g]
@@ -417,112 +395,105 @@
     def small(slot):
         return small_send, small_recv.at[slot]
 
-    @pl.loop(0, CH // 2)
-    def _(p):
+    for p in range(CH // 2):
         pieces = []
         for a in range(2):
             c = 2 * p + a
-            normalize(0, c, load_cells(pair_ref, c))
+            x = load_cells(pair_ref, c)
+            pt_ref[c] = x.astype(bf16)
+            normalize(0, c, x)
             pieces.append(factors_of(0, c, 0))
         put_halves(big_send.at[0], p, pieces)
-
-    pl.semaphore_wait(barrier, D - 1 + nz)
-
-    @pl.when(core == 1)
-    def _():
-        pl.semaphore_wait(stagger, 1)
-
-    send_all(*big(0, 0), 0)
-    second_group(0)
-    send_all(*big(0, 1), 1)
+        if p == 0:
+            pl.semaphore_wait(barrier, D - 1 + nz)
+        send_part(*big(0, 0), 0, p)
+    second_group(0, *big(0, 1), 1)
+    products(0, 0, 0)
     wait_sends(*big(0, 0), 0)
     wait_sends(*big(0, 1), 1)
 
-    @pl.when(core == 0)
-    def _():
-        pl.semaphore_signal(stagger, inc=1, device_id={"dp": mate}, device_id_type=MESH)
-
-    products(0, 0, 0)
-    wait_all(*small(0), 2)
-
     @pl.loop(0, CH // 2)
     def _(p):
+        wait_part(*small(0), 2, p)
         pieces = []
         for a, t in enumerate(halves(small_recv.at[0], p)):
             c = 2 * p + a
             res = finish_product(0, c, t)
-            one = (load_cells(pair_ref, c) + gate_ref[0, c] * res).astype(bf16)
+            one = (pt_ref[c].astype(f32) + gate_ref[0, c] * res).astype(bf16)
             normalize(1, c, one.astype(f32))
             pieces.append(factors_of(1, c, 0))
         put_halves(big_send.at[0], p, pieces)
-
-    send_all(*big(1, 0), 3)
-    second_group(1)
-    send_all(*big(1, 1), 4)
+        send_part(*big(1, 0), 3, p)
+
+    second_group(1, *big(1, 1), 4)
     wait_sends(*small(0), 2)
+
+    @pl.loop(0, CH)
+    def _(c):
+        ct_ref[c] = load_cells(cot_ref, c).astype(bf16)
+
     products(1, 3, 1)
     wait_sends(*big(1, 0), 3)
     wait_sends(*big(1, 1), 4)
-    wait_all(*small(1), 5)
     wait_sends(*small(1), 5)
 
     @pl.loop(0, CH // 2)
     def _(p):
+        wait_part(*small(1), 5, p)
         pieces = []
         for a, t in enumerate(halves(small_recv.at[1], p)):
             c = 2 * p + a
             finish_product(1, c, t)
-            pieces.append(back_to_product(1, c, load_cells(cot_ref, c)))
+            pieces.append(back_to_product(1, c, ct_ref[c].astype(f32)))
         put_halves(small_send, p, pieces)
-
-    send_all(*small(2), 6)
+        send_part(*small(2), 6, p)
+
     put_rows(early, 5 * C, out_grad(1))
     product_grads(1, 6, 2)
     wait_sends(*small(2), 6)
-    wait_all(*big(2, 0), 7)
 
     @pl.loop(0, CH // 2)
     def _(p):
+        wait_part(*big(2, 0), 7, p)
         back_to_factors(1, p, 0, 2)
-
-    wait_all(*big(2, 1), 8)
 
     @pl.loop(0, CH // 2)
     def _(p):
+        wait_part(*big(2, 1), 8, p)
         back_to_factors(1, p, 1, 2)
         pieces = []
         for a in range(2):
             c = 2 * p + a
-            up = (load_cells(cot_ref, c) + back_to_pair(1, c)).astype(bf16)
+            up = (ct_ref[c].astype(f32) + back_to_pair(1, c)).astype(bf16)
             up_ref[c] = up
             pieces.append(back_to_product(0, c, up.astype(f32)))
         put_halves(small_send, p, pieces)
-
-    send_all(*small(3), 9)
+        send_part(*small(3), 9, p)
+
     put_rows(early, 0, dot(dq_ref[1], z_ref[1], 1, 1))
     put_rows(early, 6 * C, out_grad(0))
     put_rows(early, 7 * C, dot(dq_ref[0, 4 * C : 5 * C], z_ref[0], 1, 1))
-    start_sum(early, early_in, 12)
+    start_sum(early, early_in, 0)
     wait_sends(*big(2, 0), 7)
     wait_sends(*big(2, 1), 8)
     product_grads(0, 9, 3)
     wait_sends(*small(3), 9)
-    sum_over_dap(early, early_in, 12, 0)
-    wait_all(*big(3, 0), 10)
+    sum_over_dap(early, early_in, 0)
 
     @pl.loop(0, CH // 2)
     def _(p):
+        wait_part(*big(3, 0), 10, p)
         back_to_factors(0, p, 0, 3)
 
     send_along_z(early, z_early, 0)
-    wait_all(*big(3, 1), 11)
 
     @pl.loop(0, CH // 2)
     def _(p):
+        wait_part(*big(3, 1), 11, p)
         back_to_factors(0, p, 1, 3)
 
     put_rows(late, 0, dot(dq_ref[0, 0 : 4 * C], z_ref[0], 1, 1))
-    start_sum(late, late_in, 13)
+    start_sum(late, late_in, 1)
 
     @pl.loop(0, CH)
     def _(c):
@@ -536,14 +507,10 @@
 
     wait_sends(*big(3, 0), 10)
     wait_sends(*big(3, 1), 11)
-    sum_over_dap(late, late_in, 13, 1)
+    sum_over_dap(late, late_in, 1)
     send_along_z(late, z_late, 1)
-    hand_round(early, z_early, early_all, 14, 0)
-    hand_round(late, z_late, late_all, 15, 1)
-    wait_round(early_all, 14)
-    wait_round(late_all, 15)
-    end_sum(early, early_in, 12, z_early, early_all, 0)
-    end_sum(late, late_in, 13, z_late, late_all, 1)
+    hand_round(early, z_early, early_all, 0)
+    hand_round(late, z_late, late_all, 1)
 
     def factors(x):
         blocks = []
@@ -554,13 +521,21 @@
                 blocks.append(jnp.transpose(part.reshape(C, C)))
         return blocks
 
+    round_copy(early_all, 0, peer_of(1), rest).wait_recv()
     first = early_all[...].astype(f32).reshape(EARLY, C) * (1.0 / N)
-    last = late_all[...].astype(f32).reshape(LATE, C) * (1.0 / N)
-    for u, x, gate in ((0, last, first[7 * C : 8 * C]), (1, first[0 : 4 * C], first[4 * C : 5 * C])):
-        for k, block in enumerate(factors(x) + [jnp.transpose(gate)]):
-            gin_ref[u, :, k * C : (k + 1) * C] = block
+    for k, block in enumerate(factors(first[0 : 4 * C]) + [jnp.transpose(first[4 * C : 5 * C])]):
+        gin_ref[1, :, k * C : (k + 1) * C] = block
+    gin_ref[0, :, 4 * C : 5 * C] = jnp.transpose(first[7 * C : 8 * C])
     gout_ref[0] = first[6 * C : 7 * C]
     gout_ref[1] = first[5 * C : 6 * C]
+
+    round_copy(late_all, 1, peer_of(1), rest).wait_recv()
+    last = late_all[...].astype(f32).reshape(LATE, C) * (1.0 / N)
+    for k, block in enumerate(factors(last)):
+        gin_ref[0, :, k * C : (k + 1) * C] = block
+
+    end_sum(early, early_in, z_early, early_all, 0)
+    end_sum(late, late_in, z_late, late_all, 1)
 
 
 def hand_over(a, b, c, x, y, z, sems):
@@ -589,16 +564,18 @@
         pltpu.VMEM((2, CH, 1, W), f32),
         pltpu.VMEM((2, C, CELLS), bf16),
         pltpu.VMEM((CH, C, W), bf16),
+        pltpu.VMEM((CH, C, W), bf16),
+        pltpu.VMEM((CH, C, W), bf16),
         pltpu.VMEM((2, C, CELLS), bf16),
         pltpu.VMEM((2, 5 * C, CELLS), bf16),
         pltpu.VMEM((2, 2, 8, N, N), bf16),
         pltpu.VMEM((8, N, N), bf16),
         pltpu.VMEM((3, N * 8, C), f32),
         pltpu.VMEM((3, N * 8, C), f32),
-        pltpu.VMEM((2, D, CH // 2, 16, W), bf16),
-        pltpu.VMEM((D, CH // 2, 16, W), bf16),
-        pltpu.VMEM((4, 2, D, CH // 2, 16, W), bf16),
-        pltpu.VMEM((4, D, CH // 2, 16, W), bf16),
+        pltpu.VMEM((2, CH // 2, D, 16, W), bf16),
+        pltpu.VMEM((CH // 2, D, 16, W), bf16),
+        pltpu.VMEM((4, 2, CH // 2, D, 16, W), bf16),
+        pltpu.VMEM((4, CH // 2, D, 16, W), bf16),
         pltpu.VMEM((D, EARLY // D, C), bf16),
         pltpu.VMEM((D, LATE // D, C), bf16),
         pltpu.VMEM((D, EARLY // D, C), bf16),
@@ -610,14 +587,16 @@
         pltpu.VMEM((nz, LATE // D // 2, C), bf16),
         pltpu.VMEM((D, EARLY // D, C), bf16),
         pltpu.VMEM((D, LATE // D, C), bf16),
-        pltpu.SemaphoreType.DMA((16, D)),
-        pltpu.SemaphoreType.DMA((16, D)),
-        pltpu.SemaphoreType.DMA((16,)),
+        pltpu.SemaphoreType.DMA((12, CH // 2)),
+        pltpu.SemaphoreType.DMA((12, CH // 2)),
+        pltpu.SemaphoreType.DMA((12, CH // 2)),
         pltpu.SemaphoreType.DMA((4,)),
         pltpu.SemaphoreType.DMA((4,)),
-        pltpu.SemaphoreType.DMA((2, nz)),
-        pltpu.SemaphoreType.DMA((2, nz)),
-        pltpu.SemaphoreType.REGULAR,
+        pltpu.SemaphoreType.DMA((2,)),
+        pltpu.SemaphoreType.DMA((4,)),
+        pltpu.SemaphoreType.DMA((4,)),
+        pltpu.SemaphoreType.DMA((2,)),
+        pltpu.SemaphoreType.DMA((2,)),
     ]
     grad, in_total, out_total = pl.pallas_call(
         functools.partial(kernel, ndp),

time: 151 us -> 136 us (0.901)
  Pallas kernels: 150 us -> 135 us
    pallas_call x1, Pallas kernels: 148 us -> 133 us  [local(): pl.pallas_call(functools.partial(kernel, ndp), out_shape=(jax.ShapeDtypeS...]
where the time goes in v4:
time: 136 us
  Pallas kernels  135 us (99%)
    pallas_call x1, Pallas kernels, local(): pl.pallas_call(functools.partial(kernel, ndp), out_shape=(jax.ShapeDtypeS...  133 us

profile of v4, /device:TPU:1, one launch (start us, length us, event | category | flops | bytes accessed | tf_op | source)
XLA Modules:
  0.0 135.6 jit_solution(1355825085575393086)
XLA Ops:
  0.6 132.6 %shard_map.76 = (bf16[12,192,128]{2,1,0:T(8,128)(2,1)}, f32[2,128,640]{2,1,0:T(8,128)}, f32[2,128,128]{2,1,0:T(8,128)}) custom-call(bf16[12,192,128]{2,1,0:T(8,128)(2,1)} %bitcast.3, bf16[12,192,128]{2,1,0:T(8,128)(2,1)} %bitcast.4, s32[1,192]{1,0:T(1,128)} %mask_ref.1, bf16[2,128,640]{2,1,0:T(8,128)(2,1)} %win_ref.1, bf16[2,128,128]{2,1,0:T(8,128)(2,1)} %wo_ref.1), custom_call_target="tpu_custom_call" | custom-call | tf_op jit(solution)/shard_map/pallas_call | solution.py:601
  133.2 2.4 %shard_map.77 = (bf16[12,192,128]{2,1,0:T(8,128)(2,1)}, f32[2,128,640]{2,1,0:T(8,128)}, f32[2,128,128]{2,1,0:T(8,128)}) custom-call(bf16[12,192,128]{2,1,0:T(8,128)(2,1)} %get-tuple-element.9.a, f32[2,128,640]{2,1,0:T(8,128)} %get-tuple-element.10.b, f32[2,128,128]{2,1,0:T(8,128)} %get-tuple-element.11.c), custom_call_target="tpu_custom_call" | custom-call | tf_op jit(solution)/shard_map/pallas_call | solution.py:617

commit v5 on v4

--- a/solution.py
+++ b/solution.py
@@ -16,7 +16,7 @@
 W = 2 * N
 CELLS = R * N
 EARLY = 8 * C
-LATE = 4 * C
+LATE = 2 * C
 FAR = (10, 6, 9, 11, 14, 2, 8, 5, 7, 13, 15, 1, 4, 3, 12)
 f32 = jnp.float32
 bf16 = jnp.bfloat16
@@ -49,7 +49,8 @@
     n_ref, inv_ref, z_ref, v_ref, sg_ref, gate_ref, res_ref, ntri_ref, itri_ref, xz_ref,
     pt_ref, ct_ref, up_ref, dres_ref, dq_ref, lm_ref, tm_ref, a_ref, b_ref,
     big_send, small_send, big_recv, small_recv,
-    early, late, early_in, late_in, half_mine, half_out, half_in, z_early, z_late, early_all, late_all,
+    early, mid, late, early_in, mid_in, late_in, half_mine, half_out, half_in,
+    z_early, z_mid, z_late, early_all, mid_all, late_all,
     ssem, rsem, lsem, gs, gr, own, core_s, core_r, zs, zr,
 ):
     me = lax.axis_index("dap")
@@ -86,7 +87,7 @@
     def _(k):
         pl.semaphore_signal(barrier, inc=1, device_id={"dp": z_peer(k)}, device_id_type=MESH)
 
-    for u in range(2):
+    def order_weights(u):
         wt = jnp.transpose(win_ref[u].astype(f32))
         pieces = []
         for t in range(2):
@@ -94,11 +95,13 @@
             for g in range(2):
                 at = slice(4 * g, 4 * g + 4)
                 pieces.append(jnp.concatenate([left[:, at], right[:, at]], 1).reshape(C, C))
-        wt = jnp.concatenate(pieces + [wt[4 * C : 5 * C]], 0)
-        wt_ref[u] = wt.astype(bf16)
-        wp_ref[u] = jnp.transpose(wt).astype(bf16)
+        wt_ref[u] = jnp.concatenate(pieces + [wt[4 * C : 5 * C]], 0).astype(bf16)
+
+    def transpose_weights(u):
+        wp_ref[u] = jnp.transpose(wt_ref[u].astype(f32)).astype(bf16)
         wot_ref[u] = jnp.transpose(wo_ref[u].astype(f32)).astype(bf16)
 
+    order_weights(0)
     count = jnp.sum(mask_ref[...].astype(f32), 1, keepdims=True)
 
     def cell_mask(c):
@@ -279,11 +282,11 @@
 
     def product_grads(u, phase, slot):
         unpack(2, small_send, small_recv.at[slot], phase)
-        for ch in range(8):
-            a, b = get_channel(2, ch)
-            tm_ref[ch, :, 0:C] = a
-            tm_ref[ch, :, C:N] = b
         for g in range(2):
+            for ch in range(4 * g, 4 * g + 4):
+                a, b = get_channel(2, ch)
+                tm_ref[ch, :, 0:C] = a
+                tm_ref[ch, :, C:N] = b
             for e in range(4):
                 left, right, grad = lm_ref[u, g, e], lm_ref[u, g, 4 + e], tm_ref[4 * g + e]
                 if u == 0:
@@ -326,38 +329,43 @@
     def round_copy(everyone, n, peer, slot):
         return pltpu.make_async_remote_copy(
             src_ref=everyone.at[slot], dst_ref=everyone.at[slot],
-            send_sem=gs.at[2 + n], recv_sem=gr.at[2 + n],
+            send_sem=gs.at[3 + n], recv_sem=gr.at[3 + n],
             device_id={"dap": peer}, device_id_type=MESH,
         )
 
     rest = pl.ds(0, D - 1)
     rest_z = pl.ds(0, nz - 1)
+
+    def shared(rows, n):
+        return rows.shape[1] // 2 if n == 0 else rows.shape[1]
 
     def own_half(rows):
         half = rows.shape[1] // 2
         return pl.ds(pl.multiple_of(core * half, half), half)
 
-    def swap_halves(rows, n):
-        half = rows.shape[1] // 2
-        return mate_copy(half_out.at[n, pl.ds(0, half)], half_in.at[n, pl.ds(0, half)], n)
+    def swap_rows(rows, n):
+        at = pl.ds(0, shared(rows, n))
+        return mate_copy(half_out.at[n, at], half_in.at[n, at], n)
 
     def sum_over_dap(rows, arrived, n):
-        half = rows.shape[1] // 2
         own_rows(rows, arrived, n).wait()
         sum_copy(rows, arrived, n, rest, rest, peer_of(1)).wait_recv()
-
-        def add(k, acc):
-            return acc + arrived[k].astype(f32)
-
-        total = lax.fori_loop(1, D, add, arrived[0].astype(f32))
-        half_mine[n, 0:half] = jnp.where(core == 0, total[:half], total[half:])
-        half_out[n, 0:half] = jnp.where(core == 0, total[half:], total[:half])
-        swap_halves(rows, n).start()
+        total = arrived[0].astype(f32)
+        for k in range(1, D):
+            total = total + arrived[k].astype(f32)
+        mine, theirs = total, total
+        size = shared(rows, n)
+        if n == 0:
+            mine = jnp.where(core == 0, total[:size], total[size:])
+            theirs = jnp.where(core == 0, total[size:], total[:size])
+        half_mine[n, 0:size] = mine
+        half_out[n, 0:size] = theirs
+        swap_rows(rows, n).start()
 
     def send_along_z(rows, zbuf, n):
-        half = rows.shape[1] // 2
-        swap_halves(rows, n).wait_recv()
-        zbuf[zed] = (half_mine[n, 0:half] + half_in[n, 0:half]).astype(bf16)
+        size = shared(rows, n)
+        swap_rows(rows, n).wait_recv()
+        zbuf[zed] = (half_mine[n, 0:size] + half_in[n, 0:size]).astype(bf16)
 
         @pl.loop(1, nz)
         def _(k):
@@ -367,15 +375,18 @@
         if nz > 1:
             z_copy(zbuf, n, z_peer(1), rest_z).wait_recv()
 
-        def add(k, acc):
-            return acc + zbuf[k].astype(f32)
-
-        total = lax.fori_loop(1, nz, add, zbuf[0].astype(f32)).astype(bf16)
-        mine = own_half(rows)
-        everyone[me, mine] = total
-        back = mate_copy(everyone.at[me, mine], everyone.at[me, mine], 2 + n)
-        back.start()
-        back.wait_recv()
+        total = zbuf[0].astype(f32)
+        for k in range(1, nz):
+            total = total + zbuf[k].astype(f32)
+        total = total.astype(bf16)
+        if n == 0:
+            mine = own_half(rows)
+            everyone[me, mine] = total
+            back = mate_copy(everyone.at[me, mine], everyone.at[me, mine], 3)
+            back.start()
+            back.wait_recv()
+        else:
+            everyone[me] = total
 
         @pl.loop(1, D)
         def _(k):
@@ -384,8 +395,9 @@
     def end_sum(rows, arrived, zbuf, everyone, n):
         sum_copy(rows, arrived, n, rest, rest, peer_of(1)).wait_send()
         round_copy(everyone, n, peer_of(1), rest).wait_send()
-        swap_halves(rows, n).wait_send()
-        mate_copy(everyone.at[me, own_half(rows)], everyone.at[me, own_half(rows)], 2 + n).wait_send()
+        swap_rows(rows, n).wait_send()
+        if n == 0:
+            mate_copy(everyone.at[me, own_half(rows)], everyone.at[me, own_half(rows)], 3).wait_send()
         if nz > 1:
             z_copy(zbuf, n, z_peer(1), rest_z).wait_send()
 
@@ -408,6 +420,9 @@
             pl.semaphore_wait(barrier, D - 1 + nz)
         send_part(*big(0, 0), 0, p)
     second_group(0, *big(0, 1), 1)
+    order_weights(1)
+    transpose_weights(0)
+    transpose_weights(1)
     products(0, 0, 0)
     wait_sends(*big(0, 0), 0)
     wait_sends(*big(0, 1), 1)
@@ -449,6 +464,7 @@
         send_part(*small(2), 6, p)
 
     put_rows(early, 5 * C, out_grad(1))
+    put_rows(early, 4 * C, dot(dq_ref[1, 4 * C : 5 * C], z_ref[1], 1, 1))
     product_grads(1, 6, 2)
     wait_sends(*small(2), 6)
 
@@ -456,6 +472,9 @@
     def _(p):
         wait_part(*big(2, 0), 7, p)
         back_to_factors(1, p, 0, 2)
+
+    for t in range(2):
+        put_rows(early, 2 * t * C, dot(dq_ref[1, 2 * t * C : (2 * t + 1) * C], z_ref[1], 1, 1))
 
     @pl.loop(0, CH // 2)
     def _(p):
@@ -470,7 +489,9 @@
         put_halves(small_send, p, pieces)
         send_part(*small(3), 9, p)
 
-    put_rows(early, 0, dot(dq_ref[1], z_ref[1], 1, 1))
+    for t in range(2):
+        r = (2 * t + 1) * C
+        put_rows(early, r, dot(dq_ref[1, r : r + C], z_ref[1], 1, 1))
     put_rows(early, 6 * C, out_grad(0))
     put_rows(early, 7 * C, dot(dq_ref[0, 4 * C : 5 * C], z_ref[0], 1, 1))
     start_sum(early, early_in, 0)
@@ -486,14 +507,19 @@
         back_to_factors(0, p, 0, 3)
 
     send_along_z(early, z_early, 0)
+    put_rows(mid, 0, dot(dq_ref[0, 0:C], z_ref[0], 1, 1))
+    put_rows(mid, C, dot(dq_ref[0, 2 * C : 3 * C], z_ref[0], 1, 1))
+    start_sum(mid, mid_in, 1)
 
     @pl.loop(0, CH // 2)
     def _(p):
         wait_part(*big(3, 1), 11, p)
         back_to_factors(0, p, 1, 3)
 
-    put_rows(late, 0, dot(dq_ref[0, 0 : 4 * C], z_ref[0], 1, 1))
-    start_sum(late, late_in, 1)
+    put_rows(late, 0, dot(dq_ref[0, C : 2 * C], z_ref[0], 1, 1))
+    put_rows(late, C, dot(dq_ref[0, 3 * C : 4 * C], z_ref[0], 1, 1))
+    start_sum(late, late_in, 2)
+    sum_over_dap(mid, mid_in, 1)
 
     @pl.loop(0, CH)
     def _(c):
@@ -505,12 +531,14 @@
         out_ref[i, C:N] = y[2 * C : 2 * C + 64]
         out_ref[i + 1, C:N] = y[2 * C + 64 : W]
 
+    send_along_z(mid, z_mid, 1)
+    sum_over_dap(late, late_in, 2)
+    send_along_z(late, z_late, 2)
     wait_sends(*big(3, 0), 10)
     wait_sends(*big(3, 1), 11)
-    sum_over_dap(late, late_in, 1)
-    send_along_z(late, z_late, 1)
     hand_round(early, z_early, early_all, 0)
-    hand_round(late, z_late, late_all, 1)
+    hand_round(mid, z_mid, mid_all, 1)
+    hand_round(late, z_late, late_all, 2)
 
     def factors(x):
         blocks = []
@@ -529,13 +557,16 @@
     gout_ref[0] = first[6 * C : 7 * C]
     gout_ref[1] = first[5 * C : 6 * C]
 
-    round_copy(late_all, 1, peer_of(1), rest).wait_recv()
-    last = late_all[...].astype(f32).reshape(LATE, C) * (1.0 / N)
+    round_copy(mid_all, 1, peer_of(1), rest).wait_recv()
+    round_copy(late_all, 2, peer_of(1), rest).wait_recv()
+    groups = [x[...].astype(f32).reshape(LATE, C) * (1.0 / N) for x in (mid_all, late_all)]
+    last = jnp.concatenate([x[t * C : (t + 1) * C] for t in range(2) for x in groups], 0)
     for k, block in enumerate(factors(last)):
         gin_ref[0, :, k * C : (k + 1) * C] = block
 
     end_sum(early, early_in, z_early, early_all, 0)
-    end_sum(late, late_in, z_late, late_all, 1)
+    end_sum(mid, mid_in, z_mid, mid_all, 1)
+    end_sum(late, late_in, z_late, late_all, 2)
 
 
 def hand_over(a, b, c, x, y, z, sems):
@@ -578,25 +609,29 @@
         pltpu.VMEM((4, CH // 2, D, 16, W), bf16),
         pltpu.VMEM((D, EARLY // D, C), bf16),
         pltpu.VMEM((D, LATE // D, C), bf16),
+        pltpu.VMEM((D, LATE // D, C), bf16),
         pltpu.VMEM((D, EARLY // D, C), bf16),
         pltpu.VMEM((D, LATE // D, C), bf16),
-        pltpu.VMEM((2, EARLY // D // 2, C), f32),
-        pltpu.VMEM((2, EARLY // D // 2, C), f32),
-        pltpu.VMEM((2, EARLY // D // 2, C), f32),
+        pltpu.VMEM((D, LATE // D, C), bf16),
+        pltpu.VMEM((3, EARLY // D // 2, C), f32),
+        pltpu.VMEM((3, EARLY // D // 2, C), f32),
+        pltpu.VMEM((3, EARLY // D // 2, C), f32),
         pltpu.VMEM((nz, EARLY // D // 2, C), bf16),
-        pltpu.VMEM((nz, LATE // D // 2, C), bf16),
+        pltpu.VMEM((nz, LATE // D, C), bf16),
+        pltpu.VMEM((nz, LATE // D, C), bf16),
         pltpu.VMEM((D, EARLY // D, C), bf16),
+        pltpu.VMEM((D, LATE // D, C), bf16),
         pltpu.VMEM((D, LATE // D, C), bf16),
         pltpu.SemaphoreType.DMA((12, CH // 2)),
         pltpu.SemaphoreType.DMA((12, CH // 2)),
         pltpu.SemaphoreType.DMA((12, CH // 2)),
+        pltpu.SemaphoreType.DMA((6,)),
+        pltpu.SemaphoreType.DMA((6,)),
+        pltpu.SemaphoreType.DMA((3,)),
         pltpu.SemaphoreType.DMA((4,)),
         pltpu.SemaphoreType.DMA((4,)),
-        pltpu.SemaphoreType.DMA((2,)),
-        pltpu.SemaphoreType.DMA((4,)),
-        pltpu.SemaphoreType.DMA((4,)),
-        pltpu.SemaphoreType.DMA((2,)),
-        pltpu.SemaphoreType.DMA((2,)),
+        pltpu.SemaphoreType.DMA((3,)),
+        pltpu.SemaphoreType.DMA((3,)),
     ]
     grad, in_total, out_total = pl.pallas_call(
         functools.partial(kernel, ndp),

time: 136 us -> 134 us (0.985)
  Pallas kernels: 135 us -> 133 us
    pallas_call x1, Pallas kernels: 133 us -> 131 us  [local(): pl.pallas_call(functools.partial(kernel, ndp), out_shape=(jax.ShapeDtypeS...]
where the time goes in v5:
time: 134 us
  Pallas kernels  133 us (99%)
    pallas_call x1, Pallas kernels, local(): pl.pallas_call(functools.partial(kernel, ndp), out_shape=(jax.ShapeDtypeS...  131 us

profile of v5, /device:TPU:1, one launch (start us, length us, event | category | flops | bytes accessed | tf_op | source)
XLA Modules:
  0.0 133.7 jit_solution(9721673019813395577)
XLA Ops:
  0.6 130.7 %shard_map.76 = (bf16[12,192,128]{2,1,0:T(8,128)(2,1)}, f32[2,128,640]{2,1,0:T(8,128)}, f32[2,128,128]{2,1,0:T(8,128)}) custom-call(bf16[12,192,128]{2,1,0:T(8,128)(2,1)} %bitcast.3, bf16[12,192,128]{2,1,0:T(8,128)(2,1)} %bitcast.4, s32[1,192]{1,0:T(1,128)} %mask_ref.1, bf16[2,128,640]{2,1,0:T(8,128)(2,1)} %win_ref.1, bf16[2,128,128]{2,1,0:T(8,128)(2,1)} %wo_ref.1), custom_call_target="tpu_custom_call" | custom-call | tf_op jit(solution)/shard_map/pallas_call | solution.py:636
  131.3 2.4 %shard_map.77 = (bf16[12,192,128]{2,1,0:T(8,128)(2,1)}, f32[2,128,640]{2,1,0:T(8,128)}, f32[2,128,128]{2,1,0:T(8,128)}) custom-call(bf16[12,192,128]{2,1,0:T(8,128)(2,1)} %get-tuple-element.9.a, f32[2,128,640]{2,1,0:T(8,128)} %get-tuple-element.10.b, f32[2,128,128]{2,1,0:T(8,128)} %get-tuple-element.11.c), custom_call_target="tpu_custom_call" | custom-call | tf_op jit(solution)/shard_map/pallas_call | solution.py:652

commit v6 on v5

--- a/solution.py
+++ b/solution.py
@@ -601,8 +601,8 @@
         pltpu.VMEM((2, 5 * C, CELLS), bf16),
         pltpu.VMEM((2, 2, 8, N, N), bf16),
         pltpu.VMEM((8, N, N), bf16),
-        pltpu.VMEM((3, N * 8, C), f32),
-        pltpu.VMEM((3, N * 8, C), f32),
+        pltpu.VMEM((3, N * 8 + 8, C), f32),
+        pltpu.VMEM((3, N * 8 + 8, C), f32),
         pltpu.VMEM((2, CH // 2, D, 16, W), bf16),
         pltpu.VMEM((CH // 2, D, 16, W), bf16),
         pltpu.VMEM((4, 2, CH // 2, D, 16, W), bf16),

time: 134 us -> 135 us (level)
  no operation moved by 1% of the time
where the time goes in v6:
time: 135 us
  Pallas kernels  134 us (99%)
    pallas_call x1, Pallas kernels, local(): pl.pallas_call(functools.partial(kernel, ndp), out_shape=(jax.ShapeDtypeS...  132 us

profile of v6, /device:TPU:1, one launch (start us, length us, event | category | flops | bytes accessed | tf_op | source)
XLA Modules:
  0.0 134.6 jit_solution(13696694358078124061)
XLA Ops:
  0.6 131.6 %shard_map.76 = (bf16[12,192,128]{2,1,0:T(8,128)(2,1)}, f32[2,128,640]{2,1,0:T(8,128)}, f32[2,128,128]{2,1,0:T(8,128)}) custom-call(bf16[12,192,128]{2,1,0:T(8,128)(2,1)} %bitcast.3, bf16[12,192,128]{2,1,0:T(8,128)(2,1)} %bitcast.4, s32[1,192]{1,0:T(1,128)} %mask_ref.1, bf16[2,128,640]{2,1,0:T(8,128)(2,1)} %win_ref.1, bf16[2,128,128]{2,1,0:T(8,128)(2,1)} %wo_ref.1), custom_call_target="tpu_custom_call" | custom-call | tf_op jit(solution)/shard_map/pallas_call | solution.py:636
  132.2 2.4 %shard_map.77 = (bf16[12,192,128]{2,1,0:T(8,128)(2,1)}, f32[2,128,640]{2,1,0:T(8,128)}, f32[2,128,128]{2,1,0:T(8,128)}) custom-call(bf16[12,192,128]{2,1,0:T(8,128)(2,1)} %get-tuple-element.9.a, f32[2,128,640]{2,1,0:T(8,128)} %get-tuple-element.10.b, f32[2,128,128]{2,1,0:T(8,128)} %get-tuple-element.11.c), custom_call_target="tpu_custom_call" | custom-call | tf_op jit(solution)/shard_map/pallas_call | solution.py:652
